TPU v7x, 128 devices: a whole 4x4x4 slice. The times are simulated.
128 devices in a mesh: px: 16 (over z, x), py: 8 (over y, core).
Axes of the slice: x: 4, y: 4, z: 4, core: 2. Of those that a mesh axis runs over, the one named last changes fastest.
Arguments:
- a_tiles: bfloat16 [16384, 19, 64, 64], P(('px', 'py')), may hold values from -0.15625 to 0.15625
- a_cols: int32 [16384, 19], P(('px', 'py')), may hold values from 0 to 16383, as said below
- p_tiles: bfloat16 [16384, 64, 64], P(('px', 'py')), may hold values from -0.75 to 0.75
- aggregate: int32 [16384], P(('px', 'py')), may hold values from 0 to 2047, as said below
Outputs:
- ap_rows: bfloat16 [16384, 64, 64], P(('px', 'py'))
- coarse: float32 [2048, 64, 64], P(('px', 'py'))
Inputs may be any that keep to these rules, and one draw needn't show every extreme that they name: `a_cols`: block row g's columns lie in the rows of g's partition or of a partition beside it along px or py (partition of row g is g // 128, numbered px-major, no wrap); column 0 is g itself. `aggregate`: aggregate a is owned by partition a // 16. The 128 rows of one partition fall in aggregates of at most 2 rows for each owner, and some owner gets exactly 2 rows from every partition.
All inputs are finite; a program needn't handle non-finite values.
Results may differ from a plain program's by a relative error of at most 0.0029.
Values may be sent and summed in bfloat16 or wider, within the bound.
No kernel may reach another device: no remote copies, remote signals or barrier semaphores. Data moves between devices by JAX's collectives and lax.ppermute only.
A program may use at most 192 MiB of HBM per device.

v0:
```python
import jax
import jax.numpy as jnp
from jax import lax
from jax.sharding import PartitionSpec as P

AGG_DEV = 16


def passed_along(x, axis, by):
    peers = lax.axis_size(axis)
    pairs = [(i, i + by) for i in range(peers) if 0 <= i + by < peers]
    return lax.ppermute(x, axis, pairs)


def shards(a_tiles, a_cols, p_tiles, aggregate):
    rows = p_tiles.shape[0]
    width = p_tiles.shape[1]
    blocks = a_cols.shape[1]
    grid_x = lax.axis_size("px")
    grid_y = lax.axis_size("py")
    parts = grid_x * grid_y
    me_index = lax.axis_index("px") * grid_y + lax.axis_index("py")
    pieces = [p_tiles]
    for step in (1, -1):
        pieces.append(passed_along(p_tiles, "px", step))
    for step in (1, -1):
        pieces.append(passed_along(p_tiles, "py", step))
    pool = jnp.concatenate(pieces, axis=0)
    delta = a_cols // rows - me_index
    local = a_cols % rows
    code = jnp.where(
        delta == 0,
        0,
        jnp.where(delta == -grid_y, 1, jnp.where(delta == grid_y, 2, jnp.where(delta == -1, 3, 4))),
    )
    index = code * rows + local
    group = min(rows, 32)
    while rows % group != 0:
        group = group - 1
    pool_ids = jnp.arange(5 * rows, dtype=jnp.int32)

    def one_group(args):
        tiles, picks = args
        select = (picks.reshape(-1)[:, None] == pool_ids[None, :]).astype(jnp.bfloat16)
        ghosts = jnp.einsum("qp,pbc->qbc", select, pool, preferred_element_type=jnp.float32).astype(
            jnp.bfloat16
        )
        ghosts = ghosts.reshape(group, blocks, width, width)
        return jnp.einsum(
            "rkab,rkbc->rac", tiles, ghosts, preferred_element_type=jnp.float32
        ).astype(jnp.bfloat16)

    grouped = lax.map(
        one_group,
        (
            a_tiles.reshape(rows // group, group, blocks, width, width),
            index.reshape(rows // group, group, blocks),
        ),
    )
    ap_rows = grouped.reshape(rows, width, width)
    partial_value = jnp.einsum("rba,rbc->rac", p_tiles, ap_rows, preferred_element_type=jnp.float32)
    slots = max(2, 2 * rows // parts)
    owner = aggregate // AGG_DEV
    order_idx = jnp.arange(rows, dtype=jnp.int32)
    earlier = (owner[:, None] == owner[None, :]) & (order_idx[None, :] < order_idx[:, None])
    rank = jnp.sum(earlier.astype(jnp.int32), axis=1)
    position = owner * slots + rank
    placing = (position[:, None] == jnp.arange(parts * slots, dtype=jnp.int32)[None, :]).astype(
        jnp.float32
    )
    buffer = jnp.einsum("rp,rbc->pbc", placing, partial_value, precision=lax.Precision.HIGHEST)
    label_vals = (aggregate % AGG_DEV + 1).astype(jnp.float32)
    labels = jnp.dot(label_vals, placing, precision=lax.Precision.HIGHEST)
    tiles, tile_ids = (
        lax.all_to_all(buffer, ("px", "py"), split_axis=0, concat_axis=0, tiled=True),
        lax.all_to_all(labels, ("px", "py"), split_axis=0, concat_axis=0, tiled=True),
    )
    targets = jnp.arange(AGG_DEV, dtype=jnp.float32) + 1.0
    onehot = (tile_ids[None, :] == targets[:, None]).astype(jnp.float32)
    coarse = jnp.einsum("as,sbc->abc", onehot, tiles, precision=lax.Precision.HIGHEST)
    return (ap_rows, coarse)


def solution(mesh):
    return jax.shard_map(
        shards,
        mesh=mesh,
        in_specs=(
            P(("px", "py"), None, None, None),
            P(("px", "py"), None),
            P(("px", "py"), None, None),
            P(("px", "py")),
        ),
        out_specs=(P(("px", "py"), None, None), P(("px", "py"), None, None)),
        check_vma=False,
    )
```

profile of v0, /device:TPU:1, one launch (start us, length us, event | category | flops | bytes accessed | tf_op | source)
XLA Modules:
  0.0 364.5 jit_solution(7404239886021915449)
XLA Ops:
  0.6 5.0 %collective-permute-start = (bf16[128,64,64]{0,2,1:T(8,128)(2,1)}, bf16[128,64,64]{0,2,1:T(8,128)(2,1)}, u32[]{:S(2)}, u32[]{:S(2)}) collective-permute-start(bf16[128,64,64]{0,2,1:T(8,128)(2,1)} %param.8), channel_id=1, source_target_pairs={{0,8},{8,16},{16,24},{24,32},{32,40},{40,48},{48,56},{56,64},{64,7... | collective-permute-start | bytes 3145736 | tf_op jit(solution)/shard_map/ppermute | solution.py:12
  5.6 1.3 collective-permute-start.1
  6.9 4.0 %collective-permute-start.2 = (bf16[128,64,64]{0,2,1:T(8,128)(2,1)}, bf16[128,64,64]{0,2,1:T(8,128)(2,1)S(1)}, u32[]{:S(2)}, u32[]{:S(2)}) collective-permute-start(bf16[128,64,64]{0,2,1:T(8,128)(2,1)} %param.8), channel_id=1, source_target_pairs={{0,1},{1,2},{2,3},{3,4},{4,5},{5,6},{6,7},{8,9},{9,10},{10,11},{11... | collective-permute-start | bytes 3145736 | tf_op jit(solution)/shard_map/ppermute | solution.py:12
  10.9 1.9 collective-permute-start.3
  12.9 0.7 and_select_fusion
  13.7 0.7 multiply_add_fusion
  14.4 0.6 copy-done.4
  15.0 0.8 fusion.23
  15.8 0.8 all_to_all.9
  16.6 11.9 %all-to-all-start = ((f32[128,2,1]{1,2,0:T(1,128)}), f32[128,2,1]{1,2,0:T(1,128)}, u32[]{:S(2)}, u32[]{:S(2)}) async-start(f32[128,2,1]{1,2,0:T(1,128)} %bitcast.5), calls=%async_computation | async-start | bytes 131072 | tf_op jit(solution)/shard_map/all_to_all | solution.py:76
  28.5 4.7 %copy.31 = bf16[128,64,64]{2,1,0:T(8,128)(2,1)} copy(bf16[128,64,64]{0,2,1:T(8,128)(2,1)} %param.8) | data formatting | bytes 2097152 | tf_op args[2]
  33.2 0.7 fusion.30
  34.0 54.4 %copy.27 = bf16[128,19,64,64]{3,2,1,0:T(8,128)(2,1)} copy(bf16[128,19,64,64]{0,3,2,1:T(8,128)(2,1)} %param.6) | data formatting | bytes 39845888 | tf_op args[0]
  88.6 1.5 constant_dynamic-update-slice_fusion.3
  90.1 1.5 constant_dynamic-update-slice_fusion.2
  92.1 2.3 copy-done.3
  94.5 142.0 %while.11 = (s32[]{:T(128)}, bf16[4,32,64,64]{3,2,1,0:T(8,128)(2,1)}, bf16[4,32,19,64,64]{4,3,2,1,0:T(8,128)(2,1)}, s32[4,32,19]{2,1,0:T(8,128)S(1)}, bf16[640,64,64]{0,2,1:T(8,128)(2,1)}, /*index=5*/s32[]{:T(128)}) while((s32[]{:T(128)}, bf16[4,32,64,64]{3,2,1,0:T(8,128)(2,1)}, bf16[4,32,19,64,64]{4,3,2,1,0:T(8,128)(2,1)}, ...), condition=%wide.region_1.2_spmd.clone, body=%wide.region_0.1_spmd.clone.sunk | while | flops 3509448704 | bytes 60568520 | solution.py:53
  94.6 7.1 %fusion.57 = f32[608,4096]{0,1:S(1)} fusion(bf16[640,4096]{0,1:T(8,128)(2,1)} %bitcast.72, s32[608]{0:T(1024)S(1)} %eq.146), kind=kOutput, calls=%fused_computation.5.clone.1 | convolution fusion | flops 3188060160 | bytes 15206784 | tf_op jit(solution)/shard_map/while
  101.7 3.1 convert_element_type.32
  104.8 15.7 %copy.42 = bf16[608,64,64]{2,1,0:T(8,128)(2,1)} copy(bf16[608,64,64]{0,2,1:T(8,128)(2,1)} %convert_element_type.32) | data formatting | bytes 9961472 | tf_op jit(solution)/shard_map/while/body/eval_jaxpr/convert_element_type | solution.py:45
  120.5 9.6 %fusion.58 = bf16[4,32,64,64]{3,2,1,0:T(8,128)(2,1)} fusion(bf16[4,32,64,64]{3,2,1,0:T(8,128)(2,1)} %get-tuple-element.103, s32[]{:T(128)} %get-tuple-element.102, bf16[32,19,64,64]{3,2,1,0:T(8,128)(2,1)} %bitcast.65, bf16[4,32,19,64,64]{4,3,2,1,0:T(8,128)(2,1)} %get-tuple-element.110), kind=kOutput, calls=%fused_computation.9.clone.1 | convolution fusion | flops 318898176 | bytes 20448256 | tf_op jit(solution)/shard_map/while/body/eval_jaxpr/rkab,rkbc->rac/dot_general | solution.py:49
  130.2 6.9 %fusion.57 = f32[608,4096]{0,1:S(1)} fusion(bf16[640,4096]{0,1:T(8,128)(2,1)} %bitcast.72, s32[608]{0:T(1024)S(1)} %eq.146), kind=kOutput, calls=%fused_computation.5.clone.1 | convolution fusion | flops 3188060160 | bytes 15206784 | tf_op jit(solution)/shard_map/while
  137.1 3.1 convert_element_type.32
  140.3 15.7 %copy.42 = bf16[608,64,64]{2,1,0:T(8,128)(2,1)} copy(bf16[608,64,64]{0,2,1:T(8,128)(2,1)} %convert_element_type.32) | data formatting | bytes 9961472 | tf_op jit(solution)/shard_map/while/body/eval_jaxpr/convert_element_type | solution.py:45
  155.9 9.6 %fusion.58 = bf16[4,32,64,64]{3,2,1,0:T(8,128)(2,1)} fusion(bf16[4,32,64,64]{3,2,1,0:T(8,128)(2,1)} %get-tuple-element.103, s32[]{:T(128)} %get-tuple-element.102, bf16[32,19,64,64]{3,2,1,0:T(8,128)(2,1)} %bitcast.65, bf16[4,32,19,64,64]{4,3,2,1,0:T(8,128)(2,1)} %get-tuple-element.110), kind=kOutput, calls=%fused_computation.9.clone.1 | convolution fusion | flops 318898176 | bytes 20448256 | tf_op jit(solution)/shard_map/while/body/eval_jaxpr/rkab,rkbc->rac/dot_general | solution.py:49
  165.7 6.9 %fusion.57 = f32[608,4096]{0,1:S(1)} fusion(bf16[640,4096]{0,1:T(8,128)(2,1)} %bitcast.72, s32[608]{0:T(1024)S(1)} %eq.146), kind=kOutput, calls=%fused_computation.5.clone.1 | convolution fusion | flops 3188060160 | bytes 15206784 | tf_op jit(solution)/shard_map/while
  172.6 3.1 convert_element_type.32
  175.7 15.7 %copy.42 = bf16[608,64,64]{2,1,0:T(8,128)(2,1)} copy(bf16[608,64,64]{0,2,1:T(8,128)(2,1)} %convert_element_type.32) | data formatting | bytes 9961472 | tf_op jit(solution)/shard_map/while/body/eval_jaxpr/convert_element_type | solution.py:45
  191.4 9.6 %fusion.58 = bf16[4,32,64,64]{3,2,1,0:T(8,128)(2,1)} fusion(bf16[4,32,64,64]{3,2,1,0:T(8,128)(2,1)} %get-tuple-element.103, s32[]{:T(128)} %get-tuple-element.102, bf16[32,19,64,64]{3,2,1,0:T(8,128)(2,1)} %bitcast.65, bf16[4,32,19,64,64]{4,3,2,1,0:T(8,128)(2,1)} %get-tuple-element.110), kind=kOutput, calls=%fused_computation.9.clone.1 | convolution fusion | flops 318898176 | bytes 20448256 | tf_op jit(solution)/shard_map/while/body/eval_jaxpr/rkab,rkbc->rac/dot_general | solution.py:49
  201.1 6.9 %fusion.57 = f32[608,4096]{0,1:S(1)} fusion(bf16[640,4096]{0,1:T(8,128)(2,1)} %bitcast.72, s32[608]{0:T(1024)S(1)} %eq.146), kind=kOutput, calls=%fused_computation.5.clone.1 | convolution fusion | flops 3188060160 | bytes 15206784 | tf_op jit(solution)/shard_map/while
  208.1 3.1 convert_element_type.32
  211.2 15.7 %copy.42 = bf16[608,64,64]{2,1,0:T(8,128)(2,1)} copy(bf16[608,64,64]{0,2,1:T(8,128)(2,1)} %convert_element_type.32) | data formatting | bytes 9961472 | tf_op jit(solution)/shard_map/while/body/eval_jaxpr/convert_element_type | solution.py:45
  226.9 9.6 %fusion.58 = bf16[4,32,64,64]{3,2,1,0:T(8,128)(2,1)} fusion(bf16[4,32,64,64]{3,2,1,0:T(8,128)(2,1)} %get-tuple-element.103, s32[]{:T(128)} %get-tuple-element.102, bf16[32,19,64,64]{3,2,1,0:T(8,128)(2,1)} %bitcast.65, bf16[4,32,19,64,64]{4,3,2,1,0:T(8,128)(2,1)} %get-tuple-element.110), kind=kOutput, calls=%fused_computation.9.clone.1 | convolution fusion | flops 318898176 | bytes 20448256 | tf_op jit(solution)/shard_map/while/body/eval_jaxpr/rkab,rkbc->rac/dot_general | solution.py:49
  236.5 4.4 %convolution_bitcast_fusion = f32[128,64,64]{1,2,0:T(8,128)} fusion(bf16[128,64,64]{2,1,0:T(8,128)(2,1)} %bitcast.69, bf16[128,64,64]{2,1,0:T(8,128)(2,1)S(1)} %copy-done), kind=kOutput, calls=%fused_computation.15 | convolution fusion | flops 67108864 | bytes 4194304 | tf_op jit(solution)/shard_map/rba,rbc->rac/dot_general | solution.py:61
  240.9 4.5 %copy.32 = f32[128,64,64]{0,2,1:T(8,128)S(1)} copy(f32[128,64,64]{1,2,0:T(8,128)} %convolution_bitcast_fusion) | data formatting | bytes 4194304 | tf_op jit(solution)/shard_map/rba,rbc->rac/dot_general | solution.py:61
  245.4 3.8 %fusion.22 = f32[256,4096]{0,1} fusion(f32[128,4096]{0,1:T(8,128)S(1)} %bitcast.68, s32[128]{0:T(128)S(1)} %copy-done.5), kind=kOutput, calls=%fused_computation.17 | convolution fusion | flops 1610645504 | bytes 6291968
  249.3 9.1 %copy.33 = f32[256,64,64]{2,1,0:T(8,128)} copy(f32[256,64,64]{0,2,1:T(8,128)} %bitcast.67) | data formatting | bytes 8388608 | tf_op jit(solution)/shard_map/rp,rbc->pbc/dot_general | solution.py:71
  258.4 9.4 %reshape.52 = f32[128,1,8192]{2,1,0:T(1,128)} reshape(f32[256,64,64]{2,1,0:T(8,128)} %copy.33) | data formatting | bytes 8388608
  267.8 10.2 %all-to-all-start.1 = ((f32[128,1,8192]{2,1,0:T(1,128)}), f32[128,1,8192]{2,1,0:T(1,128)}, u32[]{:S(2)}, u32[]{:S(2)}) async-start(f32[128,1,8192]{2,1,0:T(1,128)} %reshape.52), calls=%async_computation.1 | async-start | bytes 8388608 | tf_op jit(solution)/shard_map/all_to_all | solution.py:75
  278.0 0.5 broadcast.65
  278.5 1.6 reduce.3
  280.3 2.9 copy.35
  283.3 47.5 %all-to-all-done.1 = f32[128,1,8192]{2,1,0:T(1,128)} async-done(((f32[128,1,8192]{2,1,0:T(1,128)}), f32[128,1,8192]{2,1,0:T(1,128)}, u32[]{:S(2)}, u32[]{:S(2)}) %all-to-all-start.1) | async-done | bytes 4194336 | tf_op jit(solution)/shard_map/all_to_all | solution.py:75
  330.8 0.5 broadcast.70
  331.3 13.8 %reduce.4 = f32[128,8192]{1,0:T(8,128)} reduce(f32[128,1,8192]{2,1,0:T(1,128)} %all-to-all-done.1, f32[]{:T(128)} %broadcast.70), dimensions={1}, to_apply=%all_to_all.11.reduce_sub_computation | reduce | bytes 8388612 | tf_op jit(solution)/shard_map/all_to_all | solution.py:75
  345.2 7.9 %reshape.53 = f32[256,64,64]{2,1,0:T(8,128)} reshape(f32[128,8192]{1,0:T(8,128)} %reduce.4) | data formatting | bytes 8388608
  353.0 10.5 %fusion.20 = f32[16,64,64]{2,0,1:T(8,128)S(1)} fusion(f32[256,64,64]{2,1,0:T(8,128)} %reshape.53, f32[256]{0:T(256)S(1)} %eq.92, f32[16]{0:T(128)S(1)} %iota_add_fusion), kind=kOutput, calls=%fused_computation.13 | convolution fusion | flops 201330688 | bytes 4457536 | tf_op jit(solution)/shard_map/as,sbc->abc/dot_general | solution.py:80
  363.6 1.0 copy.36
  (31 shorter events, 1.5 us)
Async XLA Ops:
  0.6 88.0 %collective-permute-start = (bf16[128,64,64]{0,2,1:T(8,128)(2,1)}, bf16[128,64,64]{0,2,1:T(8,128)(2,1)}, u32[]{:S(2)}, u32[]{:S(2)}) collective-permute-start(bf16[128,64,64]{0,2,1:T(8,128)(2,1)} %param.8), channel_id=1, source_target_pairs={{0,8},{8,16},{16,24},{24,32},{32,40},{40,48},{48,56},{56,64},{64,7... | collective-permute-start | bytes 3145736 | tf_op jit(solution)/shard_map/ppermute | solution.py:12
  5.6 84.5 %collective-permute-start.1 = (bf16[128,64,64]{0,2,1:T(8,128)(2,1)}, bf16[128,64,64]{0,2,1:T(8,128)(2,1)}, u32[]{:S(2)}, u32[]{:S(2)}) collective-permute-start(bf16[128,64,64]{0,2,1:T(8,128)(2,1)} %param.8), channel_id=1, source_target_pairs={{8,0},{16,8},{24,16},{32,24},{40,32},{48,40},{56,48},{64,56},{72,6... | collective-permute-start | bytes 3145736 | tf_op jit(solution)/shard_map/ppermute | solution.py:12
  6.9 84.7 %collective-permute-start.2 = (bf16[128,64,64]{0,2,1:T(8,128)(2,1)}, bf16[128,64,64]{0,2,1:T(8,128)(2,1)S(1)}, u32[]{:S(2)}, u32[]{:S(2)}) collective-permute-start(bf16[128,64,64]{0,2,1:T(8,128)(2,1)} %param.8), channel_id=1, source_target_pairs={{0,1},{1,2},{2,3},{3,4},{4,5},{5,6},{6,7},{8,9},{9,10},{10,11},{11... | collective-permute-start | bytes 3145736 | tf_op jit(solution)/shard_map/ppermute | solution.py:12
  10.9 80.9 %collective-permute-start.3 = (bf16[128,64,64]{0,2,1:T(8,128)(2,1)}, bf16[128,64,64]{0,2,1:T(8,128)(2,1)S(1)}, u32[]{:S(2)}, u32[]{:S(2)}) collective-permute-start(bf16[128,64,64]{0,2,1:T(8,128)(2,1)} %param.8), channel_id=1, source_target_pairs={{1,0},{2,1},{3,2},{4,3},{5,4},{6,5},{7,6},{9,8},{10,9},{11,10},{12... | collective-permute-start | bytes 3145736 | tf_op jit(solution)/shard_map/ppermute | solution.py:12
  14.4 0.6 copy-start.4
  16.6 251.2 %all-to-all-start = ((f32[128,2,1]{1,2,0:T(1,128)}), f32[128,2,1]{1,2,0:T(1,128)}, u32[]{:S(2)}, u32[]{:S(2)}) async-start(f32[128,2,1]{1,2,0:T(1,128)} %bitcast.5), calls=%async_computation | async-start | bytes 131072 | tf_op jit(solution)/shard_map/all_to_all | solution.py:76
  34.0 54.4 %copy-start.2 = (bf16[128,64,64]{0,2,1:T(8,128)(2,1)S(1)}, bf16[128,64,64]{0,2,1:T(8,128)(2,1)}, u32[]{:S(2)}) copy-start(bf16[128,64,64]{0,2,1:T(8,128)(2,1)} %param.8) | copy-start | bytes 3145732
  92.1 2.4 copy-start.3
  94.5 142.0 %copy-start = (bf16[128,64,64]{2,1,0:T(8,128)(2,1)S(1)}, bf16[128,64,64]{2,1,0:T(8,128)(2,1)}, u32[]{:S(2)}) copy-start(bf16[128,64,64]{2,1,0:T(8,128)(2,1)} %copy.31) | copy-start | bytes 3145732
  240.9 4.5 %copy-start.5 = (s32[128]{0:T(128)S(1)}, s32[128]{0:T(128)}, u32[]{:S(2)}) copy-start(s32[128]{0:T(128)} %copy-done.4) | copy-start | bytes 1540
  267.8 12.6 %copy-start.1 = (bf16[4,32,64,64]{3,2,1,0:T(8,128)(2,1)S(1)}, bf16[4,32,64,64]{3,2,1,0:T(8,128)(2,1)}, u32[]{:S(2)}) copy-start(bf16[4,32,64,64]{3,2,1,0:T(8,128)(2,1)} %get-tuple-element.34) | copy-start | bytes 3145732
  267.8 63.0 %all-to-all-start.1 = ((f32[128,1,8192]{2,1,0:T(1,128)}), f32[128,1,8192]{2,1,0:T(1,128)}, u32[]{:S(2)}, u32[]{:S(2)}) async-start(f32[128,1,8192]{2,1,0:T(1,128)} %reshape.52), calls=%async_computation.1 | async-start | bytes 8388608 | tf_op jit(solution)/shard_map/all_to_all | solution.py:75
where the time goes:
time: 368 us; the launch traced here: 365 us
  local copies, waits for them, and re-layouts  166 us (45%)
  matrix products  86 us (23%)
  waiting for transfers between devices  47.6 us (13%)
  starting transfers between devices  34.3 us (9%)
  other arithmetic  30.3 us (8%)
    unnamed x22, local copies, waits for them, and re-layouts  86.5 us
    convert_element_type x4, local copies, waits for them, and re-layouts, one_group(): jnp.einsum('qp,pbc->qbc', select, pool, preferred_element_type=jnp.float32)  62.6 us
    all_to_all x1, waiting for transfers between devices, shards(): lax.all_to_all(buffer, ('px', 'py'), split_axis=0, concat_axis=0, tiled=T...  47.5 us
    dot_general x4, matrix products, one_group(): jnp.einsum('rkab,rkbc->rac', tiles, ghosts, preferred_element_type=jnp.fl...  38.5 us
    while x4, matrix products  27.9 us
    all_to_all x1, other arithmetic, shards(): lax.all_to_all(buffer, ('px', 'py'), split_axis=0, concat_axis=0, tiled=T...  13.8 us
    convert_element_type x4, other arithmetic, one_group(): jnp.einsum('qp,pbc->qbc', select, pool, preferred_element_type=jnp.float32)  12.6 us
    ppermute x4, starting transfers between devices, passed_along(): return lax.ppermute(x, axis, pairs)  12.2 us
  transfers between devices with their start and end apart: 6, of which 1 were waited for; matrix products, arithmetic and copies ran while one was open for 67% of the time, Pallas kernels for 0%

commit v1 on v0

v1 whole, which is shorter than its diff:
```python
import functools

import jax
import jax.numpy as jnp
from jax import lax
from jax.experimental import pallas as pl
from jax.experimental.pallas import tpu as pltpu
from jax.sharding import PartitionSpec as P

AGG_DEV = 16
BOTH = ("px", "py")
BF = jnp.bfloat16
F32 = jnp.float32
VMEM_LIMIT = 24 * 2**20
ROWS16 = 16
SLOTS = 2
TAGS = 8
WHOLE = pl.BlockSpec(memory_space=pltpu.VMEM)
SCALARS = pl.BlockSpec(memory_space=pltpu.SMEM)
ANYWHERE = pl.BlockSpec(memory_space=pl.ANY)


def passed_along(x, axis, by):
    peers = lax.axis_size(axis)
    pairs = [(i, i + by) for i in range(peers) if 0 <= i + by < peers]
    return lax.ppermute(x, axis, pairs)


def params():
    return pltpu.CompilerParams(vmem_limit_bytes=VMEM_LIMIT)


def stacked(matrices):
    return jnp.swapaxes(jnp.stack([m.T for m in matrices]), 0, 1)


def pack_kernel(p_ref, out_ref):
    half = p_ref.shape[0] // 2
    for g in range(0, half, ROWS16):
        pairs = [
            jnp.concatenate([p_ref[g + i], p_ref[g + i + half]], axis=0) for i in range(ROWS16)
        ]
        out_ref[:, g : g + ROWS16, :] = stacked(pairs)


def pack_tiles(p_native):
    width, _, rows = p_native.shape
    return pl.pallas_call(
        pack_kernel,
        out_shape=jax.ShapeDtypeStruct((rows, width // 2, 2 * width), BF),
        compiler_params=params(),
        cost_estimate=pl.CostEstimate(flops=0, bytes_accessed=4 * 2**20, transcendentals=0),
        name="pack_tiles",
    )(p_native)


def turn_kernel(a_hbm, out_ref, a_ref, sems):
    blocks, width, _, rows = a_hbm.shape
    half = width // 2
    groups = width // ROWS16

    def fetch(k):
        return pltpu.make_async_copy(a_hbm.at[k], a_ref.at[k], sems.at[k])

    for k in range(blocks):
        fetch(k).start()

    def chunk(j, count):
        def group(g, carry):
            part = g // groups
            first = pl.multiple_of((g % groups) * ROWS16, ROWS16)
            from_b = pl.ds(pl.multiple_of(part * half, half), half)
            mats = []
            for i in range(ROWS16):
                x = a_ref[pl.ds(4 * j, count), first + i, from_b, :].reshape(count * half, rows)
                if count < 4:
                    x = jnp.concatenate([x, jnp.zeros(((4 - count) * half, rows), BF)], axis=0)
                mats.append(x)
            to = pl.ds(pl.multiple_of(part * width + first, ROWS16), ROWS16)
            out_ref[j, :, to, :] = stacked(mats)
            return carry

        lax.fori_loop(0, 2 * groups, group, 0, unroll=4)

    def full_chunk(j, carry):
        for i in range(4):
            fetch(4 * j + i).wait()
        chunk(j, 4)
        return carry

    full = blocks // 4
    lax.fori_loop(0, full, full_chunk, 0)
    for k in range(4 * full, blocks):
        fetch(k).wait()
    if blocks % 4:
        chunk(full, blocks % 4)


def turn_p_kernel(p_ref, pt_ref):
    half = p_ref.shape[0] // 2
    for g in range(0, half, ROWS16):
        low = jnp.swapaxes(p_ref[:, g : g + ROWS16, :], 0, 1)
        high = jnp.swapaxes(p_ref[:, g + half : g + half + ROWS16, :], 0, 1)
        pt_ref[:, g : g + ROWS16, :] = stacked(
            [jnp.concatenate([low[i], high[i]], axis=0) for i in range(ROWS16)]
        )


def turn_p(p_native):
    width, _, rows = p_native.shape
    return pl.pallas_call(
        turn_p_kernel,
        in_specs=[WHOLE],
        out_specs=WHOLE,
        out_shape=jax.ShapeDtypeStruct((rows, width // 2, 2 * width), BF),
        compiler_params=params(),
        cost_estimate=pl.CostEstimate(flops=0, bytes_accessed=4 * 2**20, transcendentals=0),
        name="turn_p",
    )(p_native)


def turn_blocks(a_native):
    blocks, width, _, rows = a_native.shape
    chunks = (blocks + 3) // 4
    half = width // 2
    return pl.pallas_call(
        turn_kernel,
        in_specs=[ANYWHERE],
        out_specs=WHOLE,
        out_shape=pltpu.VMEM((chunks, rows, 2 * width, 4 * half), BF),
        scratch_shapes=[pltpu.VMEM(a_native.shape, BF), pltpu.SemaphoreType.DMA((blocks,))],
        compiler_params=params(),
        cost_estimate=pl.CostEstimate(flops=0, bytes_accessed=40 * 2**20, transcendentals=0),
        name="turn_blocks",
    )(a_native)


def galerkin_kernel(
    idx_ref, pos_ref, tag_ref, a_ref, pt_ref, p0, p1, p2, p3, p4, ap_hbm, send_ref,
    ap_ref, pool, mixed, sems, ap_sem
):
    rows, half, wide = p0.shape
    blocks = idx_ref.shape[0]
    chunks = a_ref.shape[0]
    width = 2 * half
    group = mixed.shape[0]
    copies = [
        pltpu.make_async_copy(src, pool.at[pl.ds(i * rows, rows)], sems.at[i])
        for i, src in enumerate((p0, p1, p2, p3, p4))
    ]
    for copy in copies:
        copy.start()
    tiles_at = SLOTS * half
    send_ref[:, :tiles_at, :] = jnp.zeros((send_ref.shape[0], tiles_at, wide), BF)
    send_ref[:, tiles_at:, :] = tag_ref[...]
    for copy in copies:
        copy.wait()

    def keep(g):
        part = pl.ds(pl.multiple_of(g * group, group), group)
        return pltpu.make_async_copy(ap_ref.at[part], ap_hbm.at[part], ap_sem.at[g])

    left = lax.broadcasted_iota(jnp.int32, (width, wide), 1) < width
    none = jnp.zeros((half, wide), BF)

    def some_rows(g, carry):
        for i in range(group):
            r = g * group + i
            tiles = [pool[idx_ref[k, r]] for k in range(blocks)]
            ghosts = jnp.concatenate(tiles + [none] * (4 * chunks - blocks), axis=0)
            lhs = jnp.concatenate([a_ref[j, r] for j in range(chunks)], axis=1)
            prod = jnp.dot(lhs, ghosts, preferred_element_type=F32)
            mixed[i] = jnp.where(left, prod[:width], prod[width:])
        for i in range(group):
            r = g * group + i
            value = mixed[i]
            twice = value + pltpu.roll(value, width, 1)
            ap_ref[r] = twice.astype(BF)[:, :width]
            upper = jnp.where(left, twice, 0.0).astype(BF)
            lower = jnp.where(left, 0.0, twice).astype(BF)
            part = jnp.dot(
                pt_ref[r], jnp.concatenate([upper, lower], axis=0), preferred_element_type=F32
            )
            at = pos_ref[r]
            slot = pl.ds(pl.multiple_of((at % SLOTS) * half, half), half)
            send_ref[at // SLOTS, slot, :] = part.astype(BF)
        keep(g).start()
        return carry

    def kept(g, carry):
        keep(g).wait()
        return carry

    lax.fori_loop(0, rows // group, some_rows, 0)
    lax.fori_loop(0, rows // group, kept, 0)


def galerkin(index, position, tags, turned, p_turned, pieces):
    chunks, rows, wide, _ = turned.shape
    half = wide // 4
    width = 2 * half
    group = 16
    return pl.pallas_call(
        galerkin_kernel,
        in_specs=[SCALARS, SCALARS, WHOLE, WHOLE, WHOLE] + [ANYWHERE] * 5,
        out_specs=[pl.BlockSpec(memory_space=pltpu.HBM), WHOLE],
        out_shape=[
            pltpu.HBM((rows, width, width), BF),
            jax.ShapeDtypeStruct((tags.shape[0], SLOTS * half + TAGS, wide), BF),
        ],
        scratch_shapes=[
            pltpu.VMEM((rows, width, width), BF),
            pltpu.VMEM((5 * rows, half, wide), BF),
            pltpu.VMEM((group, width, wide), F32),
            pltpu.SemaphoreType.DMA((5,)),
            pltpu.SemaphoreType.DMA((rows // group,)),
        ],
        compiler_params=params(),
        cost_estimate=pl.CostEstimate(
            flops=2 * rows * wide * wide * chunks * wide, bytes_accessed=30 * 2**20, transcendentals=0
        ),
        name="galerkin",
    )(index, position, tags, pltpu.with_memory_space_constraint(turned, pltpu.VMEM), p_turned, *pieces)


def restore_kernel(ap_ref, out_ref):
    for g in range(0, ap_ref.shape[1], ROWS16):
        turned = jnp.swapaxes(ap_ref[:, g : g + ROWS16, :], 0, 1)
        for i in range(ROWS16):
            out_ref[g + i] = turned[i].T


def restore(ap):
    rows, width, _ = ap.shape
    return pl.pallas_call(
        restore_kernel,
        out_shape=jax.ShapeDtypeStruct((width, width, rows), BF),
        compiler_params=params(),
        cost_estimate=pl.CostEstimate(flops=0, bytes_accessed=8 * 2**20, transcendentals=0),
        name="restore",
    )(ap)


def sums_kernel(got_ref, out_ref):
    parts, height, wide = got_ref.shape
    half = wide // 4
    width = 2 * half
    tags = jnp.swapaxes(got_ref[:, SLOTS * half :, :], 0, 1)
    lane = lax.broadcasted_iota(jnp.int32, (parts, wide), 1) + 1
    chosen = [
        jnp.where(tags[s].astype(jnp.int32) == lane, 1.0, 0.0).T[:AGG_DEV].astype(BF)
        for s in range(SLOTS)
    ]
    chosen = jnp.concatenate(chosen, axis=1)
    for g in range(0, half, ROWS16):
        slots = [
            jnp.swapaxes(got_ref[:, s * half + g : s * half + g + ROWS16, :], 0, 1)
            for s in range(SLOTS)
        ]
        values = [
            jnp.dot(
                chosen,
                jnp.concatenate([slot[i] for slot in slots], axis=0),
                preferred_element_type=F32,
            )
            for i in range(ROWS16)
        ]
        value = jnp.swapaxes(jnp.stack(values), 0, 1)
        out_ref[:, g : g + ROWS16, :] = value[:, :, :width]
        out_ref[:, g + half : g + half + ROWS16, :] = value[:, :, width:]


def sums(got):
    parts, height, wide = got.shape
    width = wide // 2
    return pl.pallas_call(
        sums_kernel,
        in_specs=[WHOLE],
        out_specs=WHOLE,
        out_shape=jax.ShapeDtypeStruct((AGG_DEV, width, width), F32),
        compiler_params=params(),
        name="sums",
    )(got)


def shards(a_tiles, a_cols, p_tiles, aggregate):
    rows = p_tiles.shape[0]
    grid_x = lax.axis_size("px")
    grid_y = lax.axis_size("py")
    parts = grid_x * grid_y
    me_index = lax.axis_index("px") * grid_y + lax.axis_index("py")

    p_native = jnp.transpose(p_tiles, (1, 2, 0))
    tiles = pack_tiles(p_native)
    p_turned = turn_p(p_native)
    pieces = [tiles]
    for axis in ("py", "px"):
        for step in (1, -1):
            pieces.append(passed_along(tiles, axis, step))

    cols = a_cols.T
    delta = cols // rows - me_index
    code = jnp.where(
        delta == 0,
        0,
        jnp.where(delta == -1, 1, jnp.where(delta == 1, 2, jnp.where(delta == -grid_y, 3, 4))),
    )
    index = code * rows + cols % rows

    owner = aggregate // AGG_DEV
    order = jnp.arange(rows, dtype=jnp.int32)
    earlier = (owner[:, None] == owner[None, :]) & (order[None, :] < order[:, None])
    rank = jnp.sum(earlier.astype(jnp.int32), axis=1)
    position = owner * SLOTS + rank
    spots = jnp.arange(parts * SLOTS, dtype=jnp.int32)
    placing = position[:, None] == spots[None, :]
    label = jnp.sum(jnp.where(placing, (aggregate % AGG_DEV + 1)[:, None], 0), axis=0)
    label = jnp.pad(label.astype(BF).reshape(parts, SLOTS), ((0, 0), (0, TAGS - SLOTS)))
    tags = jnp.broadcast_to(label[:, :, None], (parts, TAGS, 2 * p_tiles.shape[1]))

    a_native = jnp.transpose(a_tiles, (1, 2, 3, 0))
    a_native, index, position, tags, p_turned = lax.optimization_barrier(
        (a_native, index, position, tags, p_turned)
    )
    turned = turn_blocks(a_native)
    ap, send = galerkin(index, position, tags, turned, p_turned, pieces)
    got = lax.all_to_all(send, BOTH, split_axis=0, concat_axis=0, tiled=True)
    ap_native = restore(ap)
    coarse = sums(got)
    return (jnp.transpose(ap_native, (2, 0, 1)), coarse)


def solution(mesh):
    return jax.shard_map(
        shards,
        mesh=mesh,
        in_specs=(
            P(BOTH, None, None, None),
            P(BOTH, None),
            P(BOTH, None, None),
            P(BOTH),
        ),
        out_specs=(P(BOTH, None, None), P(BOTH, None, None)),
        check_vma=False,
    )
```

time: 368 us -> 93.5 us (0.25)
  local copies, waits for them, and re-layouts: 166 us -> 4.56 us
  matrix products: 86 us -> 0 us
  other arithmetic: 30.3 us -> 0.34 us
  Pallas kernels: 0 us -> 28.3 us
  waiting for transfers between devices: 47.6 us -> 30.7 us
  starting transfers between devices: 34.3 us -> 28.4 us
    unnamed x22 -> x10, local copies, waits for them, and re-layouts: 86.5 us -> 4.19 us
    convert_element_type x4 -> x1, local copies, waits for them, and re-layouts: 62.6 us -> 0.16 us  [shards(): label.astype(BF).reshape(parts, SLOTS)]
    dot_general x7 -> x0, matrix products: 54.2 us -> none  [the longest x4 38.5 us: one_group(): jnp.einsum('rkab,rkbc->rac', tiles, ghosts, preferred_element_type=jnp.fl...]
    pallas_call x0 -> x6, Pallas kernels: none -> 28.3 us  [the longest x1 12.1 us: galerkin(): pl.pallas_call(galerkin_kernel, in_specs=[SCALARS, SCALARS, WHOLE, WHOLE,...]
    while x4 -> x0, matrix products: 27.9 us -> none
    all_to_all x2 -> x1, waiting for transfers between devices: 47.5 us -> 29.7 us  [shards(): got = lax.all_to_all(send, BOTH, split_axis=0, concat_axis=0, tiled=True)]
    all_to_all x2 -> x0, other arithmetic: 15.5 us -> none  [the longest x1 13.8 us: shards(): lax.all_to_all(buffer, ('px', 'py'), split_axis=0, concat_axis=0, tiled=T...]
    dot_general x2 -> x0, local copies, waits for them, and re-layouts: 13.7 us -> none  [the longest x1 9.14 us: shards(): jnp.einsum('rp,rbc->pbc', placing, partial_value, precision=lax.Precision...]
  transfers between devices with their start and end apart: 6 -> 5, of which waited for: 1 -> 3; matrix products, arithmetic and copies ran while one was open for 67% -> 1% of each run, Pallas kernels for 0% -> 15%
where the time goes in v1:
time: 93.5 us; the launch traced here: 93.1 us
  waiting for transfers between devices  30.7 us (33%)
  starting transfers between devices  28.4 us (30%)
  Pallas kernels  28.3 us (30%)
  local copies, waits for them, and re-layouts  4.56 us (5%)
    all_to_all x1, waiting for transfers between devices, shards(): got = lax.all_to_all(send, BOTH, split_axis=0, concat_axis=0, tiled=True)  29.7 us
    all_to_all x1, starting transfers between devices, shards(): got = lax.all_to_all(send, BOTH, split_axis=0, concat_axis=0, tiled=True)  15.1 us
    ppermute x4, starting transfers between devices, passed_along(): return lax.ppermute(x, axis, pairs)  13.3 us
    pallas_call x1, Pallas kernels, galerkin(): pl.pallas_call(galerkin_kernel, in_specs=[SCALARS, SCALARS, WHOLE, WHOLE,...  12.1 us
    pallas_call x1, Pallas kernels, turn_blocks(): pl.pallas_call(turn_kernel, in_specs=[ANYWHERE], out_specs=WHOLE, out_sha...  11.3 us
    unnamed x10, local copies, waits for them, and re-layouts  4.19 us
    pallas_call x1, Pallas kernels, restore(): pl.pallas_call(restore_kernel, out_shape=jax.ShapeDtypeStruct((width, wid...  1.97 us
  transfers between devices with their start and end apart: 5, of which 3 were waited for; matrix products, arithmetic and copies ran while one was open for 1% of the time, Pallas kernels for 15%

profile of v1, /device:TPU:1, one launch (start us, length us, event | category | flops | bytes accessed | tf_op | source)
XLA Modules:
  0.0 93.1 jit_solution(6590587414551850126)
XLA Ops:
  0.6 0.0 copy-start.4
  0.6 0.0 copy-start
  0.7 1.2 %copy-done = bf16[128,64,64]{0,2,1:T(8,128)(2,1)S(1)} copy-done((bf16[128,64,64]{0,2,1:T(8,128)(2,1)S(1)}, bf16[128,64,64]{0,2,1:T(8,128)(2,1)}, u32[]{:S(2)}) %copy-start) | copy-done | bytes 1048600
  1.9 0.0 copy-start.3
  1.9 0.5 pack_tiles.1.p0
  2.4 1.3 %collective-permute-start.3 = (bf16[128,32,128]{2,1,0:T(8,128)(2,1)S(1)}, bf16[128,32,128]{2,1,0:T(8,128)(2,1)S(1)}, u32[]{:S(2)}, u32[]{:S(2)}) collective-permute-start(bf16[128,32,128]{2,1,0:T(8,128)(2,1)S(1)} %pack_tiles.1.p0), channel_id=1, source_target_pairs={{8,0},{16,8},{24,16},{32,24},{40,32},{48,40},{56,48},{64,56},{72,6... | collective-permute-start | bytes 3145736 | tf_op jit(solution)/shard_map/ppermute | solution.py:26
  3.7 5.5 %collective-permute-start.2 = (bf16[128,32,128]{2,1,0:T(8,128)(2,1)S(1)}, bf16[128,32,128]{2,1,0:T(8,128)(2,1)}, u32[]{:S(2)}, u32[]{:S(2)}) collective-permute-start(bf16[128,32,128]{2,1,0:T(8,128)(2,1)S(1)} %pack_tiles.1.p0), channel_id=1, source_target_pairs={{0,8},{8,16},{16,24},{24,32},{32,40},{40,48},{48,56},{56,64},{64,7... | collective-permute-start | bytes 3145736 | tf_op jit(solution)/shard_map/ppermute | solution.py:26
  9.2 3.3 %collective-permute-start.1 = (bf16[128,32,128]{2,1,0:T(8,128)(2,1)S(1)}, bf16[128,32,128]{2,1,0:T(8,128)(2,1)}, u32[]{:S(2)}, u32[]{:S(2)}) collective-permute-start(bf16[128,32,128]{2,1,0:T(8,128)(2,1)S(1)} %pack_tiles.1.p0), channel_id=1, source_target_pairs={{1,0},{2,1},{3,2},{4,3},{5,4},{6,5},{7,6},{9,8},{10,9},{11,10},{12... | collective-permute-start | bytes 3145736 | tf_op jit(solution)/shard_map/ppermute | solution.py:26
  12.5 3.2 %collective-permute-start = (bf16[128,32,128]{2,1,0:T(8,128)(2,1)S(1)}, bf16[128,32,128]{2,1,0:T(8,128)(2,1)}, u32[]{:S(2)}, u32[]{:S(2)}) collective-permute-start(bf16[128,32,128]{2,1,0:T(8,128)(2,1)S(1)} %pack_tiles.1.p0), channel_id=1, source_target_pairs={{0,1},{1,2},{2,3},{3,4},{4,5},{5,6},{6,7},{8,9},{9,10},{10,11},{11... | collective-permute-start | bytes 3145736 | tf_op jit(solution)/shard_map/ppermute | solution.py:26
  15.7 0.8 turn_p.1.pt_ref
  16.5 0.0 copy-done.4
  16.6 0.2 convert_reduce_fusion
  16.7 0.1 select_reduce_fusion
  16.9 0.2 convert_element_type.14
  17.1 0.0 copy-done.3
  17.1 0.2 broadcast_in_dim.44.tag_ref
  17.3 11.3 %turn_blocks.1.a_ref = bf16[5,128,128,128]{3,2,1,0:T(8,128)(2,1)S(1)} custom-call(bf16[19,64,64,128]{3,2,1,0:T(8,128)(2,1)} %bitcast.23), custom_call_target="tpu_custom_call" | custom-call | bytes 41943040 | tf_op jit(solution)/shard_map/turn_blocks/pallas_call | solution.py:126
  28.6 0.1 collective-permute-done.3.p4
  28.7 0.9 collective-permute-done.2.p3
  29.6 0.0 collective-permute-done.1.p2
  29.6 0.0 collective-permute-done.p1
  29.6 12.1 %galerkin.1 = (bf16[128,64,64]{2,1,0:T(8,128)(2,1)}, bf16[128,72,128]{2,1,0:T(8,128)(2,1)S(1)}) custom-call(s32[19,128]{1,0:T(8,128)S(1)} %fusion.2.idx_ref, s32[128]{0:T(128)S(1)} %multiply_add_fusion.pos_ref, bf16[128,8,128]{2,1,0:T(8,128)(2,1)S(1)} %broadcast_in_dim.44.tag_ref, bf16[5,128,128,128]{3,2,1,0:T(8,128)(2,1)S(1)} %turn_blocks.1.a_ref, ...), custom_call_target="tpu_custom_call" | custom-call | flops 2684354560 | bytes 31457280 | tf_op jit(solution)/shard_map/galerkin/pallas_call | solution.py:203
  41.6 0.0 copy-start.1
  41.7 1.4 %copy-done.1 = bf16[128,72,128]{2,1,0:T(8,128)(2,1)} copy-done((bf16[128,72,128]{2,1,0:T(8,128)(2,1)}, bf16[128,72,128]{2,1,0:T(8,128)(2,1)S(1)}, u32[]{:S(2)}) %copy-start.1) | copy-done | bytes 2359320
  43.0 15.1 %all-to-all-start = ((bf16[128,72,128]{2,1,0:T(8,128)(2,1)}), bf16[128,72,128]{2,1,0:T(8,128)(2,1)S(1)}, u32[]{:S(2)}, u32[]{:S(2)}) async-start(bf16[128,72,128]{2,1,0:T(8,128)(2,1)} %copy-done.1), calls=%async_computation | async-start | bytes 4718592 | tf_op jit(solution)/shard_map/all_to_all | solution.py:327
  58.1 0.0 copy-start.2
  58.1 1.6 %copy-done.2 = bf16[128,64,64]{2,1,0:T(8,128)(2,1)S(1)} copy-done((bf16[128,64,64]{2,1,0:T(8,128)(2,1)S(1)}, bf16[128,64,64]{2,1,0:T(8,128)(2,1)}, u32[]{:S(2)}) %copy-start.2) | copy-done | bytes 1048600
  59.7 2.0 %restore.1 = bf16[64,64,128]{2,1,0:T(8,128)(2,1)} custom-call(bf16[128,64,64]{2,1,0:T(8,128)(2,1)S(1)} %copy-done.2), custom_call_target="tpu_custom_call" | custom-call | bytes 8388608 | tf_op jit(solution)/shard_map/restore/pallas_call | solution.py:235
  61.7 29.7 %all-to-all-done.got_ref = bf16[128,72,128]{2,1,0:T(8,128)(2,1)S(1)} async-done(((bf16[128,72,128]{2,1,0:T(8,128)(2,1)}), bf16[128,72,128]{2,1,0:T(8,128)(2,1)S(1)}, u32[]{:S(2)}, u32[]{:S(2)}) %all-to-all-start) | async-done | bytes 2359328 | tf_op jit(solution)/shard_map/all_to_all | solution.py:327
  91.4 1.7 %sums.1 = f32[16,64,64]{2,1,0:T(8,128)} custom-call(bf16[128,72,128]{2,1,0:T(8,128)(2,1)S(1)} %all-to-all-done.got_ref), custom_call_target="tpu_custom_call" | custom-call | tf_op jit(solution)/shard_map/sums/pallas_call | solution.py:276
  (5 shorter events, 0.1 us)
Async XLA Ops:
  0.6 15.9 %copy-start.4 = (s32[128]{0:T(128)S(1)}, s32[128]{0:T(128)}, u32[]{:S(2)}) copy-start(s32[128]{0:T(128)} %param.7) | copy-start | bytes 1540
  0.6 1.2 %copy-start = (bf16[128,64,64]{0,2,1:T(8,128)(2,1)S(1)}, bf16[128,64,64]{0,2,1:T(8,128)(2,1)}, u32[]{:S(2)}) copy-start(bf16[128,64,64]{0,2,1:T(8,128)(2,1)} %param.6) | copy-start | bytes 3145732
  1.9 15.2 %copy-start.3 = (s32[128,19]{0,1:T(8,128)S(1)}, s32[128,19]{0,1:T(8,128)}, u32[]{:S(2)}) copy-start(s32[128,19]{0,1:T(8,128)} %param.5) | copy-start | bytes 29188
  2.4 26.3 %collective-permute-start.3 = (bf16[128,32,128]{2,1,0:T(8,128)(2,1)S(1)}, bf16[128,32,128]{2,1,0:T(8,128)(2,1)S(1)}, u32[]{:S(2)}, u32[]{:S(2)}) collective-permute-start(bf16[128,32,128]{2,1,0:T(8,128)(2,1)S(1)} %pack_tiles.1.p0), channel_id=1, source_target_pairs={{8,0},{16,8},{24,16},{32,24},{40,32},{48,40},{56,48},{64,56},{72,6... | collective-permute-start | bytes 3145736 | tf_op jit(solution)/shard_map/ppermute | solution.py:26
  3.7 25.9 %collective-permute-start.2 = (bf16[128,32,128]{2,1,0:T(8,128)(2,1)S(1)}, bf16[128,32,128]{2,1,0:T(8,128)(2,1)}, u32[]{:S(2)}, u32[]{:S(2)}) collective-permute-start(bf16[128,32,128]{2,1,0:T(8,128)(2,1)S(1)} %pack_tiles.1.p0), channel_id=1, source_target_pairs={{0,8},{8,16},{16,24},{24,32},{32,40},{40,48},{48,56},{56,64},{64,7... | collective-permute-start | bytes 3145736 | tf_op jit(solution)/shard_map/ppermute | solution.py:26
  9.2 20.4 %collective-permute-start.1 = (bf16[128,32,128]{2,1,0:T(8,128)(2,1)S(1)}, bf16[128,32,128]{2,1,0:T(8,128)(2,1)}, u32[]{:S(2)}, u32[]{:S(2)}) collective-permute-start(bf16[128,32,128]{2,1,0:T(8,128)(2,1)S(1)} %pack_tiles.1.p0), channel_id=1, source_target_pairs={{1,0},{2,1},{3,2},{4,3},{5,4},{6,5},{7,6},{9,8},{10,9},{11,10},{12... | collective-permute-start | bytes 3145736 | tf_op jit(solution)/shard_map/ppermute | solution.py:26
  12.5 17.1 %collective-permute-start = (bf16[128,32,128]{2,1,0:T(8,128)(2,1)S(1)}, bf16[128,32,128]{2,1,0:T(8,128)(2,1)}, u32[]{:S(2)}, u32[]{:S(2)}) collective-permute-start(bf16[128,32,128]{2,1,0:T(8,128)(2,1)S(1)} %pack_tiles.1.p0), channel_id=1, source_target_pairs={{0,1},{1,2},{2,3},{3,4},{4,5},{5,6},{6,7},{8,9},{9,10},{10,11},{11... | collective-permute-start | bytes 3145736 | tf_op jit(solution)/shard_map/ppermute | solution.py:26
  41.6 1.4 %copy-start.1 = (bf16[128,72,128]{2,1,0:T(8,128)(2,1)}, bf16[128,72,128]{2,1,0:T(8,128)(2,1)S(1)}, u32[]{:S(2)}) copy-start(bf16[128,72,128]{2,1,0:T(8,128)(2,1)S(1)} %get-tuple-element.15) | copy-start | bytes 7077892
  43.0 48.4 %all-to-all-start = ((bf16[128,72,128]{2,1,0:T(8,128)(2,1)}), bf16[128,72,128]{2,1,0:T(8,128)(2,1)S(1)}, u32[]{:S(2)}, u32[]{:S(2)}) async-start(bf16[128,72,128]{2,1,0:T(8,128)(2,1)} %copy-done.1), calls=%async_computation | async-start | bytes 4718592 | tf_op jit(solution)/shard_map/all_to_all | solution.py:327
  58.1 1.6 %copy-start.2 = (bf16[128,64,64]{2,1,0:T(8,128)(2,1)S(1)}, bf16[128,64,64]{2,1,0:T(8,128)(2,1)}, u32[]{:S(2)}) copy-start(bf16[128,64,64]{2,1,0:T(8,128)(2,1)} %get-tuple-element.14.ap_ref) | copy-start | bytes 3145732

commit v2 on v1

--- a/solution.py
+++ b/solution.py
@@ -34,24 +34,11 @@
     return jnp.swapaxes(jnp.stack([m.T for m in matrices]), 0, 1)
 
 
-def pack_kernel(p_ref, out_ref):
+def packed(p_ref, g):
     half = p_ref.shape[0] // 2
-    for g in range(0, half, ROWS16):
-        pairs = [
-            jnp.concatenate([p_ref[g + i], p_ref[g + i + half]], axis=0) for i in range(ROWS16)
-        ]
-        out_ref[:, g : g + ROWS16, :] = stacked(pairs)
-
-
-def pack_tiles(p_native):
-    width, _, rows = p_native.shape
-    return pl.pallas_call(
-        pack_kernel,
-        out_shape=jax.ShapeDtypeStruct((rows, width // 2, 2 * width), BF),
-        compiler_params=params(),
-        cost_estimate=pl.CostEstimate(flops=0, bytes_accessed=4 * 2**20, transcendentals=0),
-        name="pack_tiles",
-    )(p_native)
+    return stacked(
+        [jnp.concatenate([p_ref[g + i], p_ref[g + i + half]], axis=0) for i in range(ROWS16)]
+    )
 
 
 def turn_kernel(a_hbm, out_ref, a_ref, sems):
@@ -80,7 +67,7 @@
             out_ref[j, :, to, :] = stacked(mats)
             return carry
 
-        lax.fori_loop(0, 2 * groups, group, 0, unroll=4)
+        lax.fori_loop(0, 2 * groups, group, 0, unroll=8)
 
     def full_chunk(j, carry):
         for i in range(4):
@@ -96,26 +83,27 @@
         chunk(full, blocks % 4)
 
 
-def turn_p_kernel(p_ref, pt_ref):
+def own_kernel(p_ref, own_ref):
     half = p_ref.shape[0] // 2
     for g in range(0, half, ROWS16):
+        own_ref[:, g : g + ROWS16, :] = packed(p_ref, g)
         low = jnp.swapaxes(p_ref[:, g : g + ROWS16, :], 0, 1)
         high = jnp.swapaxes(p_ref[:, g + half : g + half + ROWS16, :], 0, 1)
-        pt_ref[:, g : g + ROWS16, :] = stacked(
+        own_ref[:, g + half : g + half + ROWS16, :] = stacked(
             [jnp.concatenate([low[i], high[i]], axis=0) for i in range(ROWS16)]
         )
 
 
-def turn_p(p_native):
+def own_tiles(p_native):
     width, _, rows = p_native.shape
     return pl.pallas_call(
-        turn_p_kernel,
+        own_kernel,
         in_specs=[WHOLE],
         out_specs=WHOLE,
-        out_shape=jax.ShapeDtypeStruct((rows, width // 2, 2 * width), BF),
+        out_shape=jax.ShapeDtypeStruct((rows, width, 2 * width), BF),
         compiler_params=params(),
         cost_estimate=pl.CostEstimate(flops=0, bytes_accessed=4 * 2**20, transcendentals=0),
-        name="turn_p",
+        name="own_tiles",
     )(p_native)
 
 
@@ -136,25 +124,28 @@
 
 
 def galerkin_kernel(
-    idx_ref, pos_ref, tag_ref, a_ref, pt_ref, p0, p1, p2, p3, p4, ap_hbm, send_ref,
-    ap_ref, pool, mixed, sems, ap_sem
+    idx_ref, pos_ref, tag_ref, a_ref, own_ref, p1, p2, p3, p4, ap_hbm, send_hbm,
+    ap_ref, send_ref, pool, natives, mixed, sems, ap_sem, send_sem
 ):
-    rows, half, wide = p0.shape
+    rows, width, wide = own_ref.shape
+    half = width // 2
     blocks = idx_ref.shape[0]
     chunks = a_ref.shape[0]
-    width = 2 * half
     group = mixed.shape[0]
-    copies = [
-        pltpu.make_async_copy(src, pool.at[pl.ds(i * rows, rows)], sems.at[i])
-        for i, src in enumerate((p0, p1, p2, p3, p4))
-    ]
+    others = (p1, p2, p3, p4)
+    copies = [pltpu.make_async_copy(own_ref.at[:, pl.ds(0, half)], pool.at[pl.ds(0, rows)], sems.at[0])]
+    for i, src in enumerate(others):
+        copies.append(pltpu.make_async_copy(src, natives.at[i], sems.at[i + 1]))
     for copy in copies:
         copy.start()
     tiles_at = SLOTS * half
     send_ref[:, :tiles_at, :] = jnp.zeros((send_ref.shape[0], tiles_at, wide), BF)
     send_ref[:, tiles_at:, :] = tag_ref[...]
-    for copy in copies:
-        copy.wait()
+    for i in range(len(others)):
+        copies[i + 1].wait()
+        for g in range(0, half, ROWS16):
+            pool[(i + 1) * rows : (i + 2) * rows, g : g + ROWS16, :] = packed(natives.at[i], g)
+    copies[0].wait()
 
     def keep(g):
         part = pl.ds(pl.multiple_of(g * group, group), group)
@@ -179,7 +170,7 @@
             upper = jnp.where(left, twice, 0.0).astype(BF)
             lower = jnp.where(left, 0.0, twice).astype(BF)
             part = jnp.dot(
-                pt_ref[r], jnp.concatenate([upper, lower], axis=0), preferred_element_type=F32
+                own_ref[r, half:, :], jnp.concatenate([upper, lower], axis=0), preferred_element_type=F32
             )
             at = pos_ref[r]
             slot = pl.ds(pl.multiple_of((at % SLOTS) * half, half), half)
@@ -192,35 +183,41 @@
         return carry
 
     lax.fori_loop(0, rows // group, some_rows, 0)
+    send = pltpu.make_async_copy(send_ref, send_hbm, send_sem)
+    send.start()
+    send.wait()
     lax.fori_loop(0, rows // group, kept, 0)
 
 
-def galerkin(index, position, tags, turned, p_turned, pieces):
+def galerkin(index, position, tags, turned, own, pieces):
     chunks, rows, wide, _ = turned.shape
     half = wide // 4
     width = 2 * half
-    group = 16
+    group = 32
     return pl.pallas_call(
         galerkin_kernel,
-        in_specs=[SCALARS, SCALARS, WHOLE, WHOLE, WHOLE] + [ANYWHERE] * 5,
-        out_specs=[pl.BlockSpec(memory_space=pltpu.HBM), WHOLE],
+        in_specs=[SCALARS, SCALARS, WHOLE, WHOLE, WHOLE] + [ANYWHERE] * 4,
+        out_specs=[pl.BlockSpec(memory_space=pltpu.HBM)] * 2,
         out_shape=[
             pltpu.HBM((rows, width, width), BF),
-            jax.ShapeDtypeStruct((tags.shape[0], SLOTS * half + TAGS, wide), BF),
+            pltpu.HBM((tags.shape[0], SLOTS * half + TAGS, wide), BF),
         ],
         scratch_shapes=[
             pltpu.VMEM((rows, width, width), BF),
+            pltpu.VMEM((tags.shape[0], SLOTS * half + TAGS, wide), BF),
             pltpu.VMEM((5 * rows, half, wide), BF),
+            pltpu.VMEM((4, width, width, rows), BF),
             pltpu.VMEM((group, width, wide), F32),
             pltpu.SemaphoreType.DMA((5,)),
             pltpu.SemaphoreType.DMA((rows // group,)),
+            pltpu.SemaphoreType.DMA,
         ],
         compiler_params=params(),
         cost_estimate=pl.CostEstimate(
             flops=2 * rows * wide * wide * chunks * wide, bytes_accessed=30 * 2**20, transcendentals=0
         ),
         name="galerkin",
-    )(index, position, tags, pltpu.with_memory_space_constraint(turned, pltpu.VMEM), p_turned, *pieces)
+    )(index, position, tags, pltpu.with_memory_space_constraint(turned, pltpu.VMEM), own, *pieces)
 
 
 def restore_kernel(ap_ref, out_ref):
@@ -291,12 +288,11 @@
     me_index = lax.axis_index("px") * grid_y + lax.axis_index("py")
 
     p_native = jnp.transpose(p_tiles, (1, 2, 0))
-    tiles = pack_tiles(p_native)
-    p_turned = turn_p(p_native)
-    pieces = [tiles]
+    own = own_tiles(p_native)
+    pieces = []
     for axis in ("py", "px"):
         for step in (1, -1):
-            pieces.append(passed_along(tiles, axis, step))
+            pieces.append(passed_along(p_native, axis, step))
 
     cols = a_cols.T
     delta = cols // rows - me_index
@@ -319,11 +315,11 @@
     tags = jnp.broadcast_to(label[:, :, None], (parts, TAGS, 2 * p_tiles.shape[1]))
 
     a_native = jnp.transpose(a_tiles, (1, 2, 3, 0))
-    a_native, index, position, tags, p_turned = lax.optimization_barrier(
-        (a_native, index, position, tags, p_turned)
+    a_native, index, position, tags, own = lax.optimization_barrier(
+        (a_native, index, position, tags, own)
     )
     turned = turn_blocks(a_native)
-    ap, send = galerkin(index, position, tags, turned, p_turned, pieces)
+    ap, send = galerkin(index, position, tags, turned, own, pieces)
     got = lax.all_to_all(send, BOTH, split_axis=0, concat_axis=0, tiled=True)
     ap_native = restore(ap)
     coarse = sums(got)

time: 93.5 us -> 91.9 us (0.983)
  local copies, waits for them, and re-layouts: 4.56 us -> 3.18 us
    unnamed x10 -> x8, local copies, waits for them, and re-layouts: 4.19 us -> 2.82 us
    pallas_call x1, Pallas kernels: 12.1 us -> 13.4 us  [galerkin(): pl.pallas_call(galerkin_kernel, in_specs=[SCALARS, SCALARS, WHOLE, WHOLE,...]
  transfers between devices with their start and end apart: 5 -> 5, of which waited for: 3 -> 2; matrix products, arithmetic and copies ran while one was open for 1% -> 1% of each run, Pallas kernels for 15% -> 15%
where the time goes in v2:
time: 91.9 us; the launch traced here: 91.6 us
  waiting for transfers between devices  30.1 us (33%)
  Pallas kernels  28.8 us (31%)
  starting transfers between devices  28.3 us (31%)
  local copies, waits for them, and re-layouts  3.18 us (3%)
    all_to_all x1, waiting for transfers between devices, shards(): got = lax.all_to_all(send, BOTH, split_axis=0, concat_axis=0, tiled=True)  29.7 us
    all_to_all x1, starting transfers between devices, shards(): got = lax.all_to_all(send, BOTH, split_axis=0, concat_axis=0, tiled=True)  15 us
    pallas_call x1, Pallas kernels, galerkin(): pl.pallas_call(galerkin_kernel, in_specs=[SCALARS, SCALARS, WHOLE, WHOLE,...  13.4 us
    ppermute x4, starting transfers between devices, passed_along(): return lax.ppermute(x, axis, pairs)  13.3 us
    pallas_call x1, Pallas kernels, turn_blocks(): pl.pallas_call(turn_kernel, in_specs=[ANYWHERE], out_specs=WHOLE, out_sha...  10.5 us
    unnamed x8, local copies, waits for them, and re-layouts  2.82 us
    pallas_call x1, Pallas kernels, restore(): pl.pallas_call(restore_kernel, out_shape=jax.ShapeDtypeStruct((width, wid...  1.97 us
  transfers between devices with their start and end apart: 5, of which 2 were waited for; matrix products, arithmetic and copies ran while one was open for 1% of the time, Pallas kernels for 15%

profile of v2, /device:TPU:1, one launch (start us, length us, event | category | flops | bytes accessed | tf_op | source)
XLA Modules:
  0.0 91.6 jit_solution(13906334898005821626)
XLA Ops:
  0.6 0.0 copy-start.3
  0.6 1.3 %collective-permute-start.3 = (bf16[64,64,128]{2,1,0:T(8,128)(2,1)}, bf16[64,64,128]{2,1,0:T(8,128)(2,1)S(1)}, u32[]{:S(2)}, u32[]{:S(2)}) collective-permute-start(bf16[64,64,128]{2,1,0:T(8,128)(2,1)} %bitcast.21), channel_id=1, source_target_pairs={{8,0},{16,8},{24,16},{32,24},{40,32},{48,40},{56,48},{64,56},{72,6... | collective-permute-start | bytes 3145736 | tf_op jit(solution)/shard_map/ppermute | solution.py:26
  1.9 5.6 %collective-permute-start.2 = (bf16[64,64,128]{2,1,0:T(8,128)(2,1)}, bf16[64,64,128]{2,1,0:T(8,128)(2,1)}, u32[]{:S(2)}, u32[]{:S(2)}) collective-permute-start(bf16[64,64,128]{2,1,0:T(8,128)(2,1)} %bitcast.22), channel_id=1, source_target_pairs={{0,8},{8,16},{16,24},{24,32},{32,40},{40,48},{48,56},{56,64},{64,7... | collective-permute-start | bytes 3145736 | tf_op jit(solution)/shard_map/ppermute | solution.py:26
  7.5 3.3 %collective-permute-start.1 = (bf16[64,64,128]{2,1,0:T(8,128)(2,1)}, bf16[64,64,128]{2,1,0:T(8,128)(2,1)}, u32[]{:S(2)}, u32[]{:S(2)}) collective-permute-start(bf16[64,64,128]{2,1,0:T(8,128)(2,1)} %bitcast.23), channel_id=1, source_target_pairs={{1,0},{2,1},{3,2},{4,3},{5,4},{6,5},{7,6},{9,8},{10,9},{11,10},{12... | collective-permute-start | bytes 3145736 | tf_op jit(solution)/shard_map/ppermute | solution.py:26
  10.8 3.2 %collective-permute-start = (bf16[64,64,128]{2,1,0:T(8,128)(2,1)}, bf16[64,64,128]{2,1,0:T(8,128)(2,1)}, u32[]{:S(2)}, u32[]{:S(2)}) collective-permute-start(bf16[64,64,128]{2,1,0:T(8,128)(2,1)} %bitcast.24), channel_id=1, source_target_pairs={{0,1},{1,2},{2,3},{3,4},{4,5},{5,6},{6,7},{8,9},{9,10},{10,11},{11... | collective-permute-start | bytes 3145736 | tf_op jit(solution)/shard_map/ppermute | solution.py:26
  14.0 0.0 copy-start.1
  14.0 1.2 %copy-done.1 = bf16[128,64,64]{0,2,1:T(8,128)(2,1)S(1)} copy-done((bf16[128,64,64]{0,2,1:T(8,128)(2,1)S(1)}, bf16[128,64,64]{0,2,1:T(8,128)(2,1)}, u32[]{:S(2)}) %copy-start.1) | copy-done | bytes 1048600
  15.2 0.0 copy-start.2
  15.2 1.2 %own_tiles.1.own_ref = bf16[128,64,128]{2,1,0:T(8,128)(2,1)S(1)} custom-call(bf16[64,64,128]{2,1,0:T(8,128)(2,1)S(1)} %bitcast.25), custom_call_target="tpu_custom_call" | custom-call | bytes 4194304 | tf_op jit(solution)/shard_map/own_tiles/pallas_call | solution.py:99
  16.4 0.0 copy-done.3
  16.5 0.2 convert_reduce_fusion
  16.6 0.1 select_reduce_fusion
  16.8 0.2 convert_element_type.14
  17.0 0.0 copy-done.2
  17.0 0.2 broadcast_in_dim.44.tag_ref
  17.2 10.5 %turn_blocks.1.a_ref = bf16[5,128,128,128]{3,2,1,0:T(8,128)(2,1)S(1)} custom-call(bf16[19,64,64,128]{3,2,1,0:T(8,128)(2,1)} %bitcast.26), custom_call_target="tpu_custom_call" | custom-call | bytes 41943040 | tf_op jit(solution)/shard_map/turn_blocks/pallas_call | solution.py:114
  27.7 0.0 collective-permute-done.3.p4
  27.8 0.4 collective-permute-done.2.p3
  28.2 0.0 collective-permute-done.1.p2
  28.2 0.0 collective-permute-done.p1
  28.2 13.4 %galerkin.1 = (bf16[128,64,64]{2,1,0:T(8,128)(2,1)}, bf16[128,72,128]{2,1,0:T(8,128)(2,1)}) custom-call(s32[19,128]{1,0:T(8,128)S(1)} %fusion.2.idx_ref, s32[128]{0:T(128)S(1)} %multiply_add_fusion.pos_ref, bf16[128,8,128]{2,1,0:T(8,128)(2,1)S(1)} %broadcast_in_dim.44.tag_ref, bf16[5,128,128,128]{3,2,1,0:T(8,128)(2,1)S(1)} %turn_blocks.1.a_ref, ...), custom_call_target="tpu_custom_call" | custom-call | flops 2684354560 | bytes 31457280 | tf_op jit(solution)/shard_map/galerkin/pallas_call | solution.py:197
  41.5 15.0 %all-to-all-start = ((bf16[128,72,128]{2,1,0:T(8,128)(2,1)}), bf16[128,72,128]{2,1,0:T(8,128)(2,1)S(1)}, u32[]{:S(2)}, u32[]{:S(2)}) async-start(bf16[128,72,128]{2,1,0:T(8,128)(2,1)} %get-tuple-element.15), calls=%async_computation | async-start | bytes 4718592 | tf_op jit(solution)/shard_map/all_to_all | solution.py:323
  56.5 0.0 copy-start
  56.5 1.6 %copy-done = bf16[128,64,64]{2,1,0:T(8,128)(2,1)S(1)} copy-done((bf16[128,64,64]{2,1,0:T(8,128)(2,1)S(1)}, bf16[128,64,64]{2,1,0:T(8,128)(2,1)}, u32[]{:S(2)}) %copy-start) | copy-done | bytes 1048600
  58.1 2.0 %restore.1 = bf16[64,64,128]{2,1,0:T(8,128)(2,1)} custom-call(bf16[128,64,64]{2,1,0:T(8,128)(2,1)S(1)} %copy-done), custom_call_target="tpu_custom_call" | custom-call | bytes 8388608 | tf_op jit(solution)/shard_map/restore/pallas_call | solution.py:232
  60.1 29.7 %all-to-all-done.got_ref = bf16[128,72,128]{2,1,0:T(8,128)(2,1)S(1)} async-done(((bf16[128,72,128]{2,1,0:T(8,128)(2,1)}), bf16[128,72,128]{2,1,0:T(8,128)(2,1)S(1)}, u32[]{:S(2)}, u32[]{:S(2)}) %all-to-all-start) | async-done | bytes 2359328 | tf_op jit(solution)/shard_map/all_to_all | solution.py:323
  89.8 1.7 %sums.1 = f32[16,64,64]{2,1,0:T(8,128)} custom-call(bf16[128,72,128]{2,1,0:T(8,128)(2,1)S(1)} %all-to-all-done.got_ref), custom_call_target="tpu_custom_call" | custom-call | tf_op jit(solution)/shard_map/sums/pallas_call | solution.py:273
  (5 shorter events, 0.1 us)
Async XLA Ops:
  0.6 15.8 %copy-start.3 = (s32[128]{0:T(128)S(1)}, s32[128]{0:T(128)}, u32[]{:S(2)}) copy-start(s32[128]{0:T(128)} %param.7) | copy-start | bytes 1540
  0.6 27.1 %collective-permute-start.3 = (bf16[64,64,128]{2,1,0:T(8,128)(2,1)}, bf16[64,64,128]{2,1,0:T(8,128)(2,1)S(1)}, u32[]{:S(2)}, u32[]{:S(2)}) collective-permute-start(bf16[64,64,128]{2,1,0:T(8,128)(2,1)} %bitcast.21), channel_id=1, source_target_pairs={{8,0},{16,8},{24,16},{32,24},{40,32},{48,40},{56,48},{64,56},{72,6... | collective-permute-start | bytes 3145736 | tf_op jit(solution)/shard_map/ppermute | solution.py:26
  1.9 26.2 %collective-permute-start.2 = (bf16[64,64,128]{2,1,0:T(8,128)(2,1)}, bf16[64,64,128]{2,1,0:T(8,128)(2,1)}, u32[]{:S(2)}, u32[]{:S(2)}) collective-permute-start(bf16[64,64,128]{2,1,0:T(8,128)(2,1)} %bitcast.22), channel_id=1, source_target_pairs={{0,8},{8,16},{16,24},{24,32},{32,40},{40,48},{48,56},{56,64},{64,7... | collective-permute-start | bytes 3145736 | tf_op jit(solution)/shard_map/ppermute | solution.py:26
  7.5 20.7 %collective-permute-start.1 = (bf16[64,64,128]{2,1,0:T(8,128)(2,1)}, bf16[64,64,128]{2,1,0:T(8,128)(2,1)}, u32[]{:S(2)}, u32[]{:S(2)}) collective-permute-start(bf16[64,64,128]{2,1,0:T(8,128)(2,1)} %bitcast.23), channel_id=1, source_target_pairs={{1,0},{2,1},{3,2},{4,3},{5,4},{6,5},{7,6},{9,8},{10,9},{11,10},{12... | collective-permute-start | bytes 3145736 | tf_op jit(solution)/shard_map/ppermute | solution.py:26
  10.8 17.4 %collective-permute-start = (bf16[64,64,128]{2,1,0:T(8,128)(2,1)}, bf16[64,64,128]{2,1,0:T(8,128)(2,1)}, u32[]{:S(2)}, u32[]{:S(2)}) collective-permute-start(bf16[64,64,128]{2,1,0:T(8,128)(2,1)} %bitcast.24), channel_id=1, source_target_pairs={{0,1},{1,2},{2,3},{3,4},{4,5},{5,6},{6,7},{8,9},{9,10},{10,11},{11... | collective-permute-start | bytes 3145736 | tf_op jit(solution)/shard_map/ppermute | solution.py:26
  14.0 1.2 %copy-start.1 = (bf16[128,64,64]{0,2,1:T(8,128)(2,1)S(1)}, bf16[128,64,64]{0,2,1:T(8,128)(2,1)}, u32[]{:S(2)}) copy-start(bf16[128,64,64]{0,2,1:T(8,128)(2,1)} %param.6) | copy-start | bytes 3145732
  15.2 1.7 %copy-start.2 = (s32[128,19]{0,1:T(8,128)S(1)}, s32[128,19]{0,1:T(8,128)}, u32[]{:S(2)}) copy-start(s32[128,19]{0,1:T(8,128)} %param.5) | copy-start | bytes 29188
  41.5 48.3 %all-to-all-start = ((bf16[128,72,128]{2,1,0:T(8,128)(2,1)}), bf16[128,72,128]{2,1,0:T(8,128)(2,1)S(1)}, u32[]{:S(2)}, u32[]{:S(2)}) async-start(bf16[128,72,128]{2,1,0:T(8,128)(2,1)} %get-tuple-element.15), calls=%async_computation | async-start | bytes 4718592 | tf_op jit(solution)/shard_map/all_to_all | solution.py:323
  56.5 1.6 %copy-start = (bf16[128,64,64]{2,1,0:T(8,128)(2,1)S(1)}, bf16[128,64,64]{2,1,0:T(8,128)(2,1)}, u32[]{:S(2)}) copy-start(bf16[128,64,64]{2,1,0:T(8,128)(2,1)} %get-tuple-element.14.ap_ref) | copy-start | bytes 3145732

commit v3 on v2

--- a/solution.py
+++ b/solution.py
@@ -136,12 +136,12 @@
     copies = [pltpu.make_async_copy(own_ref.at[:, pl.ds(0, half)], pool.at[pl.ds(0, rows)], sems.at[0])]
     for i, src in enumerate(others):
         copies.append(pltpu.make_async_copy(src, natives.at[i], sems.at[i + 1]))
-    for copy in copies:
+    for copy in reversed(copies):
         copy.start()
     tiles_at = SLOTS * half
     send_ref[:, :tiles_at, :] = jnp.zeros((send_ref.shape[0], tiles_at, wide), BF)
     send_ref[:, tiles_at:, :] = tag_ref[...]
-    for i in range(len(others)):
+    for i in reversed(range(len(others))):
         copies[i + 1].wait()
         for g in range(0, half, ROWS16):
             pool[(i + 1) * rows : (i + 2) * rows, g : g + ROWS16, :] = packed(natives.at[i], g)
@@ -193,7 +193,7 @@
     chunks, rows, wide, _ = turned.shape
     half = wide // 4
     width = 2 * half
-    group = 32
+    group = 64
     return pl.pallas_call(
         galerkin_kernel,
         in_specs=[SCALARS, SCALARS, WHOLE, WHOLE, WHOLE] + [ANYWHERE] * 4,

time: 91.9 us -> 91.2 us (level)
  no operation moved by 1% of the time
where the time goes in v3:
time: 91.2 us; the launch traced here: 90.9 us
  waiting for transfers between devices  30.1 us (33%)
  starting transfers between devices  28.3 us (31%)
  Pallas kernels  28.1 us (31%)
  local copies, waits for them, and re-layouts  3.18 us (3%)
    all_to_all x1, waiting for transfers between devices, shards(): got = lax.all_to_all(send, BOTH, split_axis=0, concat_axis=0, tiled=True)  29.7 us
    all_to_all x1, starting transfers between devices, shards(): got = lax.all_to_all(send, BOTH, split_axis=0, concat_axis=0, tiled=True)  15 us
    ppermute x4, starting transfers between devices, passed_along(): return lax.ppermute(x, axis, pairs)  13.3 us
    pallas_call x1, Pallas kernels, galerkin(): pl.pallas_call(galerkin_kernel, in_specs=[SCALARS, SCALARS, WHOLE, WHOLE,...  12.7 us
    pallas_call x1, Pallas kernels, turn_blocks(): pl.pallas_call(turn_kernel, in_specs=[ANYWHERE], out_specs=WHOLE, out_sha...  10.5 us
    unnamed x8, local copies, waits for them, and re-layouts  2.82 us
    pallas_call x1, Pallas kernels, restore(): pl.pallas_call(restore_kernel, out_shape=jax.ShapeDtypeStruct((width, wid...  1.97 us
  transfers between devices with their start and end apart: 5, of which 2 were waited for; matrix products, arithmetic and copies ran while one was open for 1% of the time, Pallas kernels for 15%

profile of v3, /device:TPU:1, one launch (start us, length us, event | category | flops | bytes accessed | tf_op | source)
XLA Modules:
  0.0 90.9 jit_solution(1779205134255825339)
XLA Ops:
  0.6 0.0 copy-start.3
  0.6 1.3 %collective-permute-start.3 = (bf16[64,64,128]{2,1,0:T(8,128)(2,1)}, bf16[64,64,128]{2,1,0:T(8,128)(2,1)S(1)}, u32[]{:S(2)}, u32[]{:S(2)}) collective-permute-start(bf16[64,64,128]{2,1,0:T(8,128)(2,1)} %bitcast.21), channel_id=1, source_target_pairs={{8,0},{16,8},{24,16},{32,24},{40,32},{48,40},{56,48},{64,56},{72,6... | collective-permute-start | bytes 3145736 | tf_op jit(solution)/shard_map/ppermute | solution.py:26
  1.9 5.6 %collective-permute-start.2 = (bf16[64,64,128]{2,1,0:T(8,128)(2,1)}, bf16[64,64,128]{2,1,0:T(8,128)(2,1)}, u32[]{:S(2)}, u32[]{:S(2)}) collective-permute-start(bf16[64,64,128]{2,1,0:T(8,128)(2,1)} %bitcast.22), channel_id=1, source_target_pairs={{0,8},{8,16},{16,24},{24,32},{32,40},{40,48},{48,56},{56,64},{64,7... | collective-permute-start | bytes 3145736 | tf_op jit(solution)/shard_map/ppermute | solution.py:26
  7.5 3.3 %collective-permute-start.1 = (bf16[64,64,128]{2,1,0:T(8,128)(2,1)}, bf16[64,64,128]{2,1,0:T(8,128)(2,1)}, u32[]{:S(2)}, u32[]{:S(2)}) collective-permute-start(bf16[64,64,128]{2,1,0:T(8,128)(2,1)} %bitcast.23), channel_id=1, source_target_pairs={{1,0},{2,1},{3,2},{4,3},{5,4},{6,5},{7,6},{9,8},{10,9},{11,10},{12... | collective-permute-start | bytes 3145736 | tf_op jit(solution)/shard_map/ppermute | solution.py:26
  10.8 3.2 %collective-permute-start = (bf16[64,64,128]{2,1,0:T(8,128)(2,1)}, bf16[64,64,128]{2,1,0:T(8,128)(2,1)}, u32[]{:S(2)}, u32[]{:S(2)}) collective-permute-start(bf16[64,64,128]{2,1,0:T(8,128)(2,1)} %bitcast.24), channel_id=1, source_target_pairs={{0,1},{1,2},{2,3},{3,4},{4,5},{5,6},{6,7},{8,9},{9,10},{10,11},{11... | collective-permute-start | bytes 3145736 | tf_op jit(solution)/shard_map/ppermute | solution.py:26
  14.0 0.0 copy-start.1
  14.0 1.2 %copy-done.1 = bf16[128,64,64]{0,2,1:T(8,128)(2,1)S(1)} copy-done((bf16[128,64,64]{0,2,1:T(8,128)(2,1)S(1)}, bf16[128,64,64]{0,2,1:T(8,128)(2,1)}, u32[]{:S(2)}) %copy-start.1) | copy-done | bytes 1048600
  15.2 0.0 copy-start.2
  15.2 1.2 %own_tiles.1.own_ref = bf16[128,64,128]{2,1,0:T(8,128)(2,1)S(1)} custom-call(bf16[64,64,128]{2,1,0:T(8,128)(2,1)S(1)} %bitcast.25), custom_call_target="tpu_custom_call" | custom-call | bytes 4194304 | tf_op jit(solution)/shard_map/own_tiles/pallas_call | solution.py:99
  16.4 0.0 copy-done.3
  16.5 0.2 convert_reduce_fusion
  16.6 0.1 select_reduce_fusion
  16.8 0.2 convert_element_type.14
  17.0 0.0 copy-done.2
  17.0 0.2 broadcast_in_dim.44.tag_ref
  17.2 10.5 %turn_blocks.1.a_ref = bf16[5,128,128,128]{3,2,1,0:T(8,128)(2,1)S(1)} custom-call(bf16[19,64,64,128]{3,2,1,0:T(8,128)(2,1)} %bitcast.26), custom_call_target="tpu_custom_call" | custom-call | bytes 41943040 | tf_op jit(solution)/shard_map/turn_blocks/pallas_call | solution.py:114
  27.7 0.0 collective-permute-done.3.p4
  27.8 0.4 collective-permute-done.2.p3
  28.2 0.0 collective-permute-done.1.p2
  28.2 0.0 collective-permute-done.p1
  28.2 12.7 %galerkin.1 = (bf16[128,64,64]{2,1,0:T(8,128)(2,1)}, bf16[128,72,128]{2,1,0:T(8,128)(2,1)}) custom-call(s32[19,128]{1,0:T(8,128)S(1)} %fusion.2.idx_ref, s32[128]{0:T(128)S(1)} %multiply_add_fusion.pos_ref, bf16[128,8,128]{2,1,0:T(8,128)(2,1)S(1)} %broadcast_in_dim.44.tag_ref, bf16[5,128,128,128]{3,2,1,0:T(8,128)(2,1)S(1)} %turn_blocks.1.a_ref, ...), custom_call_target="tpu_custom_call" | custom-call | flops 2684354560 | bytes 31457280 | tf_op jit(solution)/shard_map/galerkin/pallas_call | solution.py:197
  40.8 15.0 %all-to-all-start = ((bf16[128,72,128]{2,1,0:T(8,128)(2,1)}), bf16[128,72,128]{2,1,0:T(8,128)(2,1)S(1)}, u32[]{:S(2)}, u32[]{:S(2)}) async-start(bf16[128,72,128]{2,1,0:T(8,128)(2,1)} %get-tuple-element.15), calls=%async_computation | async-start | bytes 4718592 | tf_op jit(solution)/shard_map/all_to_all | solution.py:323
  55.8 0.0 copy-start
  55.8 1.6 %copy-done = bf16[128,64,64]{2,1,0:T(8,128)(2,1)S(1)} copy-done((bf16[128,64,64]{2,1,0:T(8,128)(2,1)S(1)}, bf16[128,64,64]{2,1,0:T(8,128)(2,1)}, u32[]{:S(2)}) %copy-start) | copy-done | bytes 1048600
  57.4 2.0 %restore.1 = bf16[64,64,128]{2,1,0:T(8,128)(2,1)} custom-call(bf16[128,64,64]{2,1,0:T(8,128)(2,1)S(1)} %copy-done), custom_call_target="tpu_custom_call" | custom-call | bytes 8388608 | tf_op jit(solution)/shard_map/restore/pallas_call | solution.py:232
  59.4 29.7 %all-to-all-done.got_ref = bf16[128,72,128]{2,1,0:T(8,128)(2,1)S(1)} async-done(((bf16[128,72,128]{2,1,0:T(8,128)(2,1)}), bf16[128,72,128]{2,1,0:T(8,128)(2,1)S(1)}, u32[]{:S(2)}, u32[]{:S(2)}) %all-to-all-start) | async-done | bytes 2359328 | tf_op jit(solution)/shard_map/all_to_all | solution.py:323
  89.1 1.7 %sums.1 = f32[16,64,64]{2,1,0:T(8,128)} custom-call(bf16[128,72,128]{2,1,0:T(8,128)(2,1)S(1)} %all-to-all-done.got_ref), custom_call_target="tpu_custom_call" | custom-call | tf_op jit(solution)/shard_map/sums/pallas_call | solution.py:273
  (5 shorter events, 0.1 us)
Async XLA Ops:
  0.6 15.8 %copy-start.3 = (s32[128]{0:T(128)S(1)}, s32[128]{0:T(128)}, u32[]{:S(2)}) copy-start(s32[128]{0:T(128)} %param.7) | copy-start | bytes 1540
  0.6 27.1 %collective-permute-start.3 = (bf16[64,64,128]{2,1,0:T(8,128)(2,1)}, bf16[64,64,128]{2,1,0:T(8,128)(2,1)S(1)}, u32[]{:S(2)}, u32[]{:S(2)}) collective-permute-start(bf16[64,64,128]{2,1,0:T(8,128)(2,1)} %bitcast.21), channel_id=1, source_target_pairs={{8,0},{16,8},{24,16},{32,24},{40,32},{48,40},{56,48},{64,56},{72,6... | collective-permute-start | bytes 3145736 | tf_op jit(solution)/shard_map/ppermute | solution.py:26
  1.9 26.2 %collective-permute-start.2 = (bf16[64,64,128]{2,1,0:T(8,128)(2,1)}, bf16[64,64,128]{2,1,0:T(8,128)(2,1)}, u32[]{:S(2)}, u32[]{:S(2)}) collective-permute-start(bf16[64,64,128]{2,1,0:T(8,128)(2,1)} %bitcast.22), channel_id=1, source_target_pairs={{0,8},{8,16},{16,24},{24,32},{32,40},{40,48},{48,56},{56,64},{64,7... | collective-permute-start | bytes 3145736 | tf_op jit(solution)/shard_map/ppermute | solution.py:26
  7.5 20.7 %collective-permute-start.1 = (bf16[64,64,128]{2,1,0:T(8,128)(2,1)}, bf16[64,64,128]{2,1,0:T(8,128)(2,1)}, u32[]{:S(2)}, u32[]{:S(2)}) collective-permute-start(bf16[64,64,128]{2,1,0:T(8,128)(2,1)} %bitcast.23), channel_id=1, source_target_pairs={{1,0},{2,1},{3,2},{4,3},{5,4},{6,5},{7,6},{9,8},{10,9},{11,10},{12... | collective-permute-start | bytes 3145736 | tf_op jit(solution)/shard_map/ppermute | solution.py:26
  10.8 17.4 %collective-permute-start = (bf16[64,64,128]{2,1,0:T(8,128)(2,1)}, bf16[64,64,128]{2,1,0:T(8,128)(2,1)}, u32[]{:S(2)}, u32[]{:S(2)}) collective-permute-start(bf16[64,64,128]{2,1,0:T(8,128)(2,1)} %bitcast.24), channel_id=1, source_target_pairs={{0,1},{1,2},{2,3},{3,4},{4,5},{5,6},{6,7},{8,9},{9,10},{10,11},{11... | collective-permute-start | bytes 3145736 | tf_op jit(solution)/shard_map/ppermute | solution.py:26
  14.0 1.2 %copy-start.1 = (bf16[128,64,64]{0,2,1:T(8,128)(2,1)S(1)}, bf16[128,64,64]{0,2,1:T(8,128)(2,1)}, u32[]{:S(2)}) copy-start(bf16[128,64,64]{0,2,1:T(8,128)(2,1)} %param.6) | copy-start | bytes 3145732
  15.2 1.7 %copy-start.2 = (s32[128,19]{0,1:T(8,128)S(1)}, s32[128,19]{0,1:T(8,128)}, u32[]{:S(2)}) copy-start(s32[128,19]{0,1:T(8,128)} %param.5) | copy-start | bytes 29188
  40.8 48.3 %all-to-all-start = ((bf16[128,72,128]{2,1,0:T(8,128)(2,1)}), bf16[128,72,128]{2,1,0:T(8,128)(2,1)S(1)}, u32[]{:S(2)}, u32[]{:S(2)}) async-start(bf16[128,72,128]{2,1,0:T(8,128)(2,1)} %get-tuple-element.15), calls=%async_computation | async-start | bytes 4718592 | tf_op jit(solution)/shard_map/all_to_all | solution.py:323
  55.8 1.6 %copy-start = (bf16[128,64,64]{2,1,0:T(8,128)(2,1)S(1)}, bf16[128,64,64]{2,1,0:T(8,128)(2,1)}, u32[]{:S(2)}) copy-start(bf16[128,64,64]{2,1,0:T(8,128)(2,1)} %get-tuple-element.14.ap_ref) | copy-start | bytes 3145732

commit v4 on v3

--- a/solution.py
+++ b/solution.py
@@ -165,10 +165,10 @@
         for i in range(group):
             r = g * group + i
             value = mixed[i]
-            twice = value + pltpu.roll(value, width, 1)
-            ap_ref[r] = twice.astype(BF)[:, :width]
-            upper = jnp.where(left, twice, 0.0).astype(BF)
-            lower = jnp.where(left, 0.0, twice).astype(BF)
+            twice = (value + pltpu.roll(value, width, 1)).astype(BF)
+            ap_ref[r] = twice[:, :width]
+            upper = jnp.where(left, twice, jnp.zeros_like(twice))
+            lower = jnp.where(left, jnp.zeros_like(twice), twice)
             part = jnp.dot(
                 own_ref[r, half:, :], jnp.concatenate([upper, lower], axis=0), preferred_element_type=F32
             )

time: 91.2 us -> 91.2 us (level)
  no operation moved by 1% of the time
where the time goes in v4:
time: 91.2 us; the launch traced here: 90.9 us
  waiting for transfers between devices  30.1 us (33%)
  starting transfers between devices  28.3 us (31%)
  Pallas kernels  28.1 us (31%)
  local copies, waits for them, and re-layouts  3.18 us (3%)
    all_to_all x1, waiting for transfers between devices, shards(): got = lax.all_to_all(send, BOTH, split_axis=0, concat_axis=0, tiled=True)  29.7 us
    all_to_all x1, starting transfers between devices, shards(): got = lax.all_to_all(send, BOTH, split_axis=0, concat_axis=0, tiled=True)  15 us
    ppermute x4, starting transfers between devices, passed_along(): return lax.ppermute(x, axis, pairs)  13.3 us
    pallas_call x1, Pallas kernels, galerkin(): pl.pallas_call(galerkin_kernel, in_specs=[SCALARS, SCALARS, WHOLE, WHOLE,...  12.7 us
    pallas_call x1, Pallas kernels, turn_blocks(): pl.pallas_call(turn_kernel, in_specs=[ANYWHERE], out_specs=WHOLE, out_sha...  10.5 us
    unnamed x8, local copies, waits for them, and re-layouts  2.82 us
    pallas_call x1, Pallas kernels, restore(): pl.pallas_call(restore_kernel, out_shape=jax.ShapeDtypeStruct((width, wid...  1.97 us
  transfers between devices with their start and end apart: 5, of which 2 were waited for; matrix products, arithmetic and copies ran while one was open for 1% of the time, Pallas kernels for 15%

profile of v4, /device:TPU:1, one launch (start us, length us, event | category | flops | bytes accessed | tf_op | source)
XLA Modules:
  0.0 90.9 jit_solution(8751995847301873671)
XLA Ops:
  0.6 0.0 copy-start.3
  0.6 1.3 %collective-permute-start.3 = (bf16[64,64,128]{2,1,0:T(8,128)(2,1)}, bf16[64,64,128]{2,1,0:T(8,128)(2,1)S(1)}, u32[]{:S(2)}, u32[]{:S(2)}) collective-permute-start(bf16[64,64,128]{2,1,0:T(8,128)(2,1)} %bitcast.21), channel_id=1, source_target_pairs={{8,0},{16,8},{24,16},{32,24},{40,32},{48,40},{56,48},{64,56},{72,6... | collective-permute-start | bytes 3145736 | tf_op jit(solution)/shard_map/ppermute | solution.py:26
  1.9 5.6 %collective-permute-start.2 = (bf16[64,64,128]{2,1,0:T(8,128)(2,1)}, bf16[64,64,128]{2,1,0:T(8,128)(2,1)}, u32[]{:S(2)}, u32[]{:S(2)}) collective-permute-start(bf16[64,64,128]{2,1,0:T(8,128)(2,1)} %bitcast.22), channel_id=1, source_target_pairs={{0,8},{8,16},{16,24},{24,32},{32,40},{40,48},{48,56},{56,64},{64,7... | collective-permute-start | bytes 3145736 | tf_op jit(solution)/shard_map/ppermute | solution.py:26
  7.5 3.3 %collective-permute-start.1 = (bf16[64,64,128]{2,1,0:T(8,128)(2,1)}, bf16[64,64,128]{2,1,0:T(8,128)(2,1)}, u32[]{:S(2)}, u32[]{:S(2)}) collective-permute-start(bf16[64,64,128]{2,1,0:T(8,128)(2,1)} %bitcast.23), channel_id=1, source_target_pairs={{1,0},{2,1},{3,2},{4,3},{5,4},{6,5},{7,6},{9,8},{10,9},{11,10},{12... | collective-permute-start | bytes 3145736 | tf_op jit(solution)/shard_map/ppermute | solution.py:26
  10.8 3.2 %collective-permute-start = (bf16[64,64,128]{2,1,0:T(8,128)(2,1)}, bf16[64,64,128]{2,1,0:T(8,128)(2,1)}, u32[]{:S(2)}, u32[]{:S(2)}) collective-permute-start(bf16[64,64,128]{2,1,0:T(8,128)(2,1)} %bitcast.24), channel_id=1, source_target_pairs={{0,1},{1,2},{2,3},{3,4},{4,5},{5,6},{6,7},{8,9},{9,10},{10,11},{11... | collective-permute-start | bytes 3145736 | tf_op jit(solution)/shard_map/ppermute | solution.py:26
  14.0 0.0 copy-start.1
  14.0 1.2 %copy-done.1 = bf16[128,64,64]{0,2,1:T(8,128)(2,1)S(1)} copy-done((bf16[128,64,64]{0,2,1:T(8,128)(2,1)S(1)}, bf16[128,64,64]{0,2,1:T(8,128)(2,1)}, u32[]{:S(2)}) %copy-start.1) | copy-done | bytes 1048600
  15.2 0.0 copy-start.2
  15.2 1.2 %own_tiles.1.own_ref = bf16[128,64,128]{2,1,0:T(8,128)(2,1)S(1)} custom-call(bf16[64,64,128]{2,1,0:T(8,128)(2,1)S(1)} %bitcast.25), custom_call_target="tpu_custom_call" | custom-call | bytes 4194304 | tf_op jit(solution)/shard_map/own_tiles/pallas_call | solution.py:99
  16.4 0.0 copy-done.3
  16.5 0.2 convert_reduce_fusion
  16.6 0.1 select_reduce_fusion
  16.8 0.2 convert_element_type.14
  17.0 0.0 copy-done.2
  17.0 0.2 broadcast_in_dim.44.tag_ref
  17.2 10.5 %turn_blocks.1.a_ref = bf16[5,128,128,128]{3,2,1,0:T(8,128)(2,1)S(1)} custom-call(bf16[19,64,64,128]{3,2,1,0:T(8,128)(2,1)} %bitcast.26), custom_call_target="tpu_custom_call" | custom-call | bytes 41943040 | tf_op jit(solution)/shard_map/turn_blocks/pallas_call | solution.py:114
  27.7 0.0 collective-permute-done.3.p4
  27.8 0.4 collective-permute-done.2.p3
  28.2 0.0 collective-permute-done.1.p2
  28.2 0.0 collective-permute-done.p1
  28.2 12.7 %galerkin.1 = (bf16[128,64,64]{2,1,0:T(8,128)(2,1)}, bf16[128,72,128]{2,1,0:T(8,128)(2,1)}) custom-call(s32[19,128]{1,0:T(8,128)S(1)} %fusion.2.idx_ref, s32[128]{0:T(128)S(1)} %multiply_add_fusion.pos_ref, bf16[128,8,128]{2,1,0:T(8,128)(2,1)S(1)} %broadcast_in_dim.44.tag_ref, bf16[5,128,128,128]{3,2,1,0:T(8,128)(2,1)S(1)} %turn_blocks.1.a_ref, ...), custom_call_target="tpu_custom_call" | custom-call | flops 2684354560 | bytes 31457280 | tf_op jit(solution)/shard_map/galerkin/pallas_call | solution.py:197
  40.9 15.0 %all-to-all-start = ((bf16[128,72,128]{2,1,0:T(8,128)(2,1)}), bf16[128,72,128]{2,1,0:T(8,128)(2,1)S(1)}, u32[]{:S(2)}, u32[]{:S(2)}) async-start(bf16[128,72,128]{2,1,0:T(8,128)(2,1)} %get-tuple-element.15), calls=%async_computation | async-start | bytes 4718592 | tf_op jit(solution)/shard_map/all_to_all | solution.py:323
  55.8 0.0 copy-start
  55.9 1.6 %copy-done = bf16[128,64,64]{2,1,0:T(8,128)(2,1)S(1)} copy-done((bf16[128,64,64]{2,1,0:T(8,128)(2,1)S(1)}, bf16[128,64,64]{2,1,0:T(8,128)(2,1)}, u32[]{:S(2)}) %copy-start) | copy-done | bytes 1048600
  57.4 2.0 %restore.1 = bf16[64,64,128]{2,1,0:T(8,128)(2,1)} custom-call(bf16[128,64,64]{2,1,0:T(8,128)(2,1)S(1)} %copy-done), custom_call_target="tpu_custom_call" | custom-call | bytes 8388608 | tf_op jit(solution)/shard_map/restore/pallas_call | solution.py:232
  59.4 29.7 %all-to-all-done.got_ref = bf16[128,72,128]{2,1,0:T(8,128)(2,1)S(1)} async-done(((bf16[128,72,128]{2,1,0:T(8,128)(2,1)}), bf16[128,72,128]{2,1,0:T(8,128)(2,1)S(1)}, u32[]{:S(2)}, u32[]{:S(2)}) %all-to-all-start) | async-done | bytes 2359328 | tf_op jit(solution)/shard_map/all_to_all | solution.py:323
  89.2 1.7 %sums.1 = f32[16,64,64]{2,1,0:T(8,128)} custom-call(bf16[128,72,128]{2,1,0:T(8,128)(2,1)S(1)} %all-to-all-done.got_ref), custom_call_target="tpu_custom_call" | custom-call | tf_op jit(solution)/shard_map/sums/pallas_call | solution.py:273
  (5 shorter events, 0.1 us)
Async XLA Ops:
  0.6 15.8 %copy-start.3 = (s32[128]{0:T(128)S(1)}, s32[128]{0:T(128)}, u32[]{:S(2)}) copy-start(s32[128]{0:T(128)} %param.7) | copy-start | bytes 1540
  0.6 27.1 %collective-permute-start.3 = (bf16[64,64,128]{2,1,0:T(8,128)(2,1)}, bf16[64,64,128]{2,1,0:T(8,128)(2,1)S(1)}, u32[]{:S(2)}, u32[]{:S(2)}) collective-permute-start(bf16[64,64,128]{2,1,0:T(8,128)(2,1)} %bitcast.21), channel_id=1, source_target_pairs={{8,0},{16,8},{24,16},{32,24},{40,32},{48,40},{56,48},{64,56},{72,6... | collective-permute-start | bytes 3145736 | tf_op jit(solution)/shard_map/ppermute | solution.py:26
  1.9 26.2 %collective-permute-start.2 = (bf16[64,64,128]{2,1,0:T(8,128)(2,1)}, bf16[64,64,128]{2,1,0:T(8,128)(2,1)}, u32[]{:S(2)}, u32[]{:S(2)}) collective-permute-start(bf16[64,64,128]{2,1,0:T(8,128)(2,1)} %bitcast.22), channel_id=1, source_target_pairs={{0,8},{8,16},{16,24},{24,32},{32,40},{40,48},{48,56},{56,64},{64,7... | collective-permute-start | bytes 3145736 | tf_op jit(solution)/shard_map/ppermute | solution.py:26
  7.5 20.7 %collective-permute-start.1 = (bf16[64,64,128]{2,1,0:T(8,128)(2,1)}, bf16[64,64,128]{2,1,0:T(8,128)(2,1)}, u32[]{:S(2)}, u32[]{:S(2)}) collective-permute-start(bf16[64,64,128]{2,1,0:T(8,128)(2,1)} %bitcast.23), channel_id=1, source_target_pairs={{1,0},{2,1},{3,2},{4,3},{5,4},{6,5},{7,6},{9,8},{10,9},{11,10},{12... | collective-permute-start | bytes 3145736 | tf_op jit(solution)/shard_map/ppermute | solution.py:26
  10.8 17.4 %collective-permute-start = (bf16[64,64,128]{2,1,0:T(8,128)(2,1)}, bf16[64,64,128]{2,1,0:T(8,128)(2,1)}, u32[]{:S(2)}, u32[]{:S(2)}) collective-permute-start(bf16[64,64,128]{2,1,0:T(8,128)(2,1)} %bitcast.24), channel_id=1, source_target_pairs={{0,1},{1,2},{2,3},{3,4},{4,5},{5,6},{6,7},{8,9},{9,10},{10,11},{11... | collective-permute-start | bytes 3145736 | tf_op jit(solution)/shard_map/ppermute | solution.py:26
  14.0 1.2 %copy-start.1 = (bf16[128,64,64]{0,2,1:T(8,128)(2,1)S(1)}, bf16[128,64,64]{0,2,1:T(8,128)(2,1)}, u32[]{:S(2)}) copy-start(bf16[128,64,64]{0,2,1:T(8,128)(2,1)} %param.6) | copy-start | bytes 3145732
  15.2 1.7 %copy-start.2 = (s32[128,19]{0,1:T(8,128)S(1)}, s32[128,19]{0,1:T(8,128)}, u32[]{:S(2)}) copy-start(s32[128,19]{0,1:T(8,128)} %param.5) | copy-start | bytes 29188
  40.9 48.3 %all-to-all-start = ((bf16[128,72,128]{2,1,0:T(8,128)(2,1)}), bf16[128,72,128]{2,1,0:T(8,128)(2,1)S(1)}, u32[]{:S(2)}, u32[]{:S(2)}) async-start(bf16[128,72,128]{2,1,0:T(8,128)(2,1)} %get-tuple-element.15), calls=%async_computation | async-start | bytes 4718592 | tf_op jit(solution)/shard_map/all_to_all | solution.py:323
  55.8 1.6 %copy-start = (bf16[128,64,64]{2,1,0:T(8,128)(2,1)S(1)}, bf16[128,64,64]{2,1,0:T(8,128)(2,1)}, u32[]{:S(2)}) copy-start(bf16[128,64,64]{2,1,0:T(8,128)(2,1)} %get-tuple-element.14.ap_ref) | copy-start | bytes 3145732
